TPU v7x, 512 devices: a whole 4x4x16 slice. The times are simulated.
512 devices in a mesh: pair: 128 (over x, z, core), harm: 4 (over y).
Axes of the slice: x: 4, y: 4, z: 16, core: 2. Of those that a mesh axis runs over, the one named last changes fastest.
Arguments:
- stick: int32 [256, 65536], P(None, ('pair', 'harm')), may hold values from 0 to 1, as said below
- stiffness: float32 [65536], P(('pair', 'harm')), may hold values from 0.3 to 3
- slip_tangent: float32 [256, 65536], P(None, ('pair', 'harm')), may hold values from 0.02 to 1
- contact_force: float32 [256, 65536], P(None, ('pair', 'harm')), may hold values from -6 to 6
- owner_node: int32 [2, 65536], P(None, ('pair', 'harm')), may hold values from 0 to 16383, as said below
- live_pairs: int32 [512], P(('pair', 'harm')), may hold values from 32 to 128, as said below
Outputs:
- interface_blocks: bfloat16 [67, 68, 16384], P(None, 'harm', 'pair')
Inputs may be any that keep to these rules, and one draw needn't show every extreme that they name: `stick`: each value is 0 or 1; each pair sticks at each sample independently, with a probability that is the same for one device's pairs and differs between devices. Pair p lies on device p div 128 of pair+harm (harm minor); node n is owned by device n div 32, which has the same harm index as the devices of the pairs that name it. owner_node[0, p] mod 32 is below 16 and owner_node[1, p] mod 32 is not. Of the 256 nodes named by one device's pairs (live or not), at most 3 are owned by the devices of any one pair index; in every draw, for each harm index, some pair index owns nodes named by every device of that harm index, all named by live pairs. `live_pairs`: some device has all 128 pairs live in every draw.
All inputs are finite; a program needn't handle non-finite values.
Results may differ from a plain program's by a relative error of at most 0.001.
Values may be sent and summed in bfloat16 or wider, within the bound.
No kernel may reach another device: no remote copies, remote signals or barrier semaphores. Data moves between devices by JAX's collectives and lax.ppermute only.
A program may use at most 64 MiB of HBM per device.

v0:
```python
import math

import jax
import jax.numpy as jnp
from jax import lax
from jax.sharding import PartitionSpec as P

HARMONICS = 33
NODE_DEV = 32


precise = lax.Precision.HIGHEST


def fourier_basis(samples, coef_count):
    time_index = jnp.arange(samples, dtype=jnp.int32)[:, None]
    column = jnp.arange(coef_count, dtype=jnp.int32)[None, :]
    harmonic = (column + 1) // 2
    reduced = harmonic * time_index % samples
    phase_angle = reduced.astype(jnp.float32) * (2.0 * math.pi / samples)
    use_sine = jnp.logical_and(column > 0, column % 2 == 0)
    return jnp.where(use_sine, jnp.sin(phase_angle), jnp.cos(phase_angle))


def product_table(fourier, samples):
    coef_count = fourier.shape[1]
    outer = jnp.einsum("ti,tj->ijt", fourier, fourier)
    return outer.reshape(coef_count * coef_count, samples) * (2.0 / samples)


def sandwich(table, fourier, weights, forces):
    coef_count = fourier.shape[1]
    node_count = weights.shape[1]
    stiffness_part = jnp.dot(table, weights, precision=precise)
    stiffness_part = stiffness_part.reshape(coef_count, coef_count, node_count)
    force_col = jnp.dot(fourier.T, forces, precision=precise) / math.sqrt(fourier.shape[0])
    merged = jnp.concatenate([stiffness_part, force_col[:, None, :]], axis=1)
    return merged.reshape(coef_count * (coef_count + 1), node_count)


def owner_table(arrived_ids):
    node_range = jnp.arange(NODE_DEV, dtype=jnp.float32)
    return (arrived_ids[0][:, None] == node_range[None, :]).astype(jnp.float32)


def on_device(stick, stiffness, slip_tangent, contact_force, owner_node, live_pairs):
    samples, pair_dev = stick.shape
    coef_count = 2 * HARMONICS + 1
    harm_count = lax.axis_size("harm")
    pair_count = lax.axis_size("pair")
    capacity = (12 * pair_dev + 5 * pair_count - 1) // (5 * pair_count)
    slot_count = pair_count * capacity
    send_count = 2 * pair_dev
    live_mask = (jnp.arange(pair_dev, dtype=jnp.int32) < live_pairs[0]).astype(jnp.float32)
    stick_float = stick.astype(jnp.float32)
    weights = (stiffness * live_mask)[None, :] * (stick_float + (1.0 - stick_float) * slip_tangent)
    forces = contact_force * live_mask[None, :]
    send_nodes = owner_node.reshape(send_count)
    target = send_nodes // (harm_count * NODE_DEV)
    local_node = send_nodes % NODE_DEV
    matches = (target[:, None] == jnp.arange(pair_count, dtype=jnp.int32)[None, :]).astype(
        jnp.int32
    )
    position = jnp.sum((jnp.cumsum(matches, axis=0) - matches) * matches, axis=1)
    slot_index = target * capacity + position
    source = jnp.full((slot_count,), send_count, jnp.int32)
    source = source.at[slot_index].set(jnp.arange(send_count, dtype=jnp.int32))
    filled = source < send_count
    column = jnp.where(filled, source % pair_dev, 0)
    node_id = jnp.where(filled, jnp.take(local_node, jnp.minimum(source, send_count - 1)), -1)
    node_id = node_id.astype(jnp.float32)[None, :]
    fourier = fourier_basis(samples, coef_count)
    table = product_table(fourier, samples)
    pair_block = sandwich(table, fourier, weights, forces)
    outgoing = jnp.take(pair_block, column, axis=1)
    arrived, arrived_ids = (
        lax.all_to_all(outgoing, "pair", split_axis=1, concat_axis=1, tiled=True),
        lax.all_to_all(node_id, "pair", split_axis=1, concat_axis=1, tiled=True),
    )
    summed = jnp.dot(arrived, owner_table(arrived_ids), precision=precise)
    rounded = summed.astype(jnp.bfloat16).reshape(coef_count, coef_count + 1, NODE_DEV)
    return lax.all_to_all(rounded, "harm", split_axis=1, concat_axis=2, tiled=True)


def solution(mesh):
    return jax.shard_map(
        on_device,
        mesh=mesh,
        in_specs=(
            P(None, ("pair", "harm")),
            P(("pair", "harm")),
            P(None, ("pair", "harm")),
            P(None, ("pair", "harm")),
            P(None, ("pair", "harm")),
            P(("pair", "harm")),
        ),
        out_specs=P(None, "harm", "pair"),
        check_vma=False,
    )
```

profile of v0, /device:TPU:1, one launch (start us, length us, event | category | flops | bytes accessed | tf_op | source)
XLA Modules:
  0.0 520.0 jit_solution(13896732525731978898)
XLA Ops:
  0.0 0.7 and_select_fusion.4
  0.7 0.7 and_select_fusion.1
  2.0 0.7 compare_select_fusion
  2.7 1.4 scatter_custom_fusion
  4.1 2.8 gather_fusion.1
  6.9 0.8 all_to_all.27
  7.8 20.4 %all-to-all-start.1 = ((f32[1,128,3]{2,0,1:T(1,128)}), f32[1,128,3]{2,0,1:T(1,128)S(1)}, u32[]{:S(2)}, u32[]{:S(2)}) async-start(f32[1,128,3]{2,0,1:T(1,128)} %bitcast.11), calls=%async_computation.1 | async-start | bytes 131072 | tf_op jit(solution)/shard_map/all_to_all | solution.py:78
  29.3 1.5 convolution_multiply_fusion
  31.0 0.7 compare_select_fusion.9
  31.7 5.2 fusion
  37.1 1.6 reshape.221
  38.6 2.0 copy.18
  40.7 5.1 gather_fusion
  45.8 9.8 %gather.11 = f32[4556,128,3]{0,2,1:T(4,128)} reshape(f32[4556,384]{0,1:T(8,128)} %bitcast.54) | data formatting | bytes 13996032 | tf_op jit(solution)/shard_map/jit(_take)/gather | solution.py:75
  55.5 10.4 %broadcast_select_fusion = f32[4556,128,3]{0,2,1:T(4,128)} fusion(f32[4556,128,3]{0,2,1:T(4,128)} %gather.11, pred[128,3]{1,0:T(8,128)(4,1)S(1)} %broadcast_in_dim.49), kind=kLoop, calls=%fused_computation.8 | loop fusion | flops 1749504 | bytes 13996416 | tf_op jit(solution)/shard_map/jit(_take)/select_n | solution.py:75
  66.0 16.6 %all-to-all-start = ((f32[4556,128,3]{0,2,1:T(4,128)}), f32[4556,128,3]{0,2,1:T(4,128)}, u32[]{:S(2)}, u32[]{:S(2)}) async-start(f32[4556,128,3]{0,2,1:T(4,128)} %broadcast_select_fusion), calls=%async_computation | async-start | bytes 18874368 | tf_op jit(solution)/shard_map/all_to_all | solution.py:77
  83.1 0.8 reduce.3
  84.1 406.3 %all-to-all-done = f32[4556,128,3]{0,2,1:T(4,128)} async-done(((f32[4556,128,3]{0,2,1:T(4,128)}), f32[4556,128,3]{0,2,1:T(4,128)}, u32[]{:S(2)}, u32[]{:S(2)}) %all-to-all-start) | async-done | bytes 6998048 | tf_op jit(solution)/shard_map/all_to_all | solution.py:77
  490.4 10.2 %all_to_all.26 = f32[4556,384]{0,1:T(8,128)} reshape(f32[4556,128,3]{0,2,1:T(4,128)} %all-to-all-done) | data formatting | bytes 13996032 | tf_op jit(solution)/shard_map/all_to_all | solution.py:77
  500.6 5.7 %convolution_convert_fusion = bf16[4556,32]{0,1:T(8,128)(2,1)S(1)} fusion(f32[4556,384]{0,1:T(8,128)} %all_to_all.26, f32[384]{0:T(512)S(1)} %eq.61), kind=kOutput, calls=%fused_computation.3 | convolution fusion | flops 671967616 | bytes 7291136 | tf_op jit(solution)/shard_map/dot_general | solution.py:80
  506.3 0.6 reshape.222
  506.9 1.0 copy.20
  507.9 11.1 %all_to_all.36 = bf16[67,68,32]{0,2,1:T(8,128)(2,1)S(1)} all-to-all(bf16[67,68,32]{0,2,1:T(8,128)(2,1)S(1)} %copy.20), channel_id=1, replica_groups=mesh['pair'=128,'harm'=4] {'harm'}, dimensions={1} | all-to-all | bytes 583168 | tf_op jit(solution)/shard_map/all_to_all | solution.py:82
  519.0 1.0 copy.22
  (26 shorter events, 2.2 us)
Async XLA Ops:
  7.8 58.2 %all-to-all-start.1 = ((f32[1,128,3]{2,0,1:T(1,128)}), f32[1,128,3]{2,0,1:T(1,128)S(1)}, u32[]{:S(2)}, u32[]{:S(2)}) async-start(f32[1,128,3]{2,0,1:T(1,128)} %bitcast.11), calls=%async_computation.1 | async-start | bytes 131072 | tf_op jit(solution)/shard_map/all_to_all | solution.py:78
  66.0 424.4 %all-to-all-start = ((f32[4556,128,3]{0,2,1:T(4,128)}), f32[4556,128,3]{0,2,1:T(4,128)}, u32[]{:S(2)}, u32[]{:S(2)}) async-start(f32[4556,128,3]{0,2,1:T(4,128)} %broadcast_select_fusion), calls=%async_computation | async-start | bytes 18874368 | tf_op jit(solution)/shard_map/all_to_all | solution.py:77
where the time goes:
time: 526 us; the launch traced here: 520 us
  waiting for transfers between devices  406 us (77%)
  local copies, waits for them, and re-layouts  37.4 us (7%)
  starting transfers between devices  37 us (7%)
  other arithmetic  15 us (3%)
  matrix products  12.4 us (2%)
  blocking collectives  11.1 us (2%)
    all_to_all x1, waiting for transfers between devices, on_device(): lax.all_to_all(outgoing, 'pair', split_axis=1, concat_axis=1, tiled=True)  406 us
    all_to_all x1, starting transfers between devices, on_device(): lax.all_to_all(node_id, 'pair', split_axis=1, concat_axis=1, tiled=True)  20.4 us
    all_to_all x1, starting transfers between devices, on_device(): lax.all_to_all(outgoing, 'pair', split_axis=1, concat_axis=1, tiled=True)  16.6 us
    gather x2, local copies, waits for them, and re-layouts, on_device(): outgoing = jnp.take(pair_block, column, axis=1)  14.9 us
    all_to_all x1, blocking collectives, on_device(): lax.all_to_all(rounded, 'harm', split_axis=1, concat_axis=2, tiled=True)  11.1 us
  transfers between devices with their start and end apart: 2, of which 1 were waited for; matrix products, arithmetic and copies ran while one was open for 7% of the time, Pallas kernels for 0%

commit v1 on v0

v1 whole, which is shorter than its diff:
```python
import functools
import math

import jax
import jax.numpy as jnp
import numpy as np
from jax import lax
from jax.experimental import pallas as pl
from jax.experimental.pallas import tpu as pltpu
from jax.sharding import Mesh
from jax.sharding import PartitionSpec as P

HARMONICS = 33
COEFS = 2 * HARMONICS + 1
SAMPLES = 256
NODE_DEV = 32
CAP = 3
SIZES = {"x": 4, "z": 16, "c": 2, "h": 4}
FIRST = ("x", "z")
REST = tuple(axis for axis in ("x", "z", "c") if axis not in FIRST)
N_FIRST = math.prod(SIZES[axis] for axis in FIRST)
N_REST = math.prod(SIZES[axis] for axis in REST)
N_HARM = SIZES["h"]
GROUP = -(-N_REST * CAP // 8) * 8
SLOTS = N_FIRST * GROUP

LANES = 128
W_LANES = 72
F_LOW = 34
MEAN, EXP_W, EXP_F, NODE = 112, 113, 114, 115
STEPS = 16.0
TOP = 32766.0
MEAN_PAIR = 2.0**21
MEAN_NODE = 2.0**31 / (1024.0 * CAP * N_FIRST)
PER = (COEFS + 1) // N_HARM
PAD = 72
T_ROWS = PER * PAD


def analysis_table():
    k = np.arange(HARMONICS * 2 + 1)[:, None]
    angle = (k * np.arange(SAMPLES)[None, :] % SAMPLES) * (2.0 * np.pi / SAMPLES)
    cosine, sine = np.cos(angle), np.sin(angle)
    basis = np.zeros((COEFS, SAMPLES))
    basis[0] = 1.0
    basis[1::2] = cosine[1 : HARMONICS + 1]
    basis[2::2] = sine[1 : HARMONICS + 1]
    table = np.zeros((2 * LANES, 2 * SAMPLES))
    top = 2 * HARMONICS
    table[:top, :SAMPLES] = cosine[1:]
    table[LANES : LANES + top, :SAMPLES] = sine[1:]
    table[MEAN, :SAMPLES] = 1.0
    table[W_LANES : W_LANES + F_LOW, SAMPLES:] = basis[:F_LOW]
    table[LANES + W_LANES : LANES + W_LANES + COEFS - F_LOW, SAMPLES:] = basis[F_LOW:]
    return table.astype(np.float32)


def synthesis_table():
    table = np.zeros((N_HARM, PER, PAD, 2 * LANES), np.float32)

    def add(row, kind, k, value):
        if kind == "s":
            if k == 0:
                return
            row[LANES + abs(k) - 1] += value if k > 0 else -value
        elif k == 0:
            row[MEAN] += value
        else:
            row[abs(k) - 1] += value

    for i in range(COEFS):
        a, i_sine = (i + 1) // 2, i > 0 and i % 2 == 0
        for j in range(COEFS + 1):
            row = table[j // PER, j % PER, i]
            if j == COEFS:
                lane = W_LANES + i if i < F_LOW else LANES + W_LANES + i - F_LOW
                row[lane] = 1.0 / math.sqrt(SAMPLES)
                continue
            b, j_sine = (j + 1) // 2, j > 0 and j % 2 == 0
            half = 1.0 / SAMPLES
            if i_sine and j_sine:
                add(row, "c", a - b, half)
                add(row, "c", a + b, -half)
            elif not i_sine and not j_sine:
                add(row, "c", a - b, half)
                add(row, "c", a + b, half)
            elif i_sine:
                add(row, "s", a + b, half)
                add(row, "s", a - b, half)
            else:
                add(row, "s", a + b, half)
                add(row, "s", b - a, half)
    return table.reshape(N_HARM, T_ROWS, 2 * LANES).astype(jnp.bfloat16)


def index_along(axes, part):
    index = 0
    for axis in axes:
        index = index * SIZES[axis] + part[axis]
    return index


def scale_step(largest):
    return jnp.ceil(jnp.log2(jnp.maximum(largest, 1e-30)) * STEPS + 0.01)


def send_kernel(live_ref, stick_ref, stiff_ref, slip_ref, force_ref, owner_ref, table_ref, out_ref):
    pairs = stick_ref.shape[1]
    live = (lax.broadcasted_iota(jnp.int32, (1, pairs), 1) < live_ref[0]).astype(jnp.float32)
    stick = stick_ref[...].astype(jnp.float32)
    weights = (stiff_ref[...] * live) * (stick + (1.0 - stick) * slip_ref[...])
    forces = force_ref[...] * live
    sums = jnp.dot(
        table_ref[...],
        jnp.concatenate([weights, forces], axis=0),
        precision=lax.Precision.HIGHEST,
        preferred_element_type=jnp.float32,
    )
    low, high = sums[:LANES], sums[LANES:]
    size = jnp.maximum(jnp.abs(low), jnp.abs(high))
    step_w = scale_step(jnp.max(size[:W_LANES], axis=0, keepdims=True))
    step_f = scale_step(jnp.max(size[W_LANES:MEAN], axis=0, keepdims=True))
    lane = lax.broadcasted_iota(jnp.int32, (LANES, pairs), 0)
    factor = jnp.where(
        lane < W_LANES, jnp.exp2(step_w * (-1.0 / STEPS)) * TOP, jnp.exp2(step_f * (-1.0 / STEPS)) * TOP
    )
    mean = jnp.round(sums[MEAN : MEAN + 1] * MEAN_PAIR).astype(jnp.int32)
    low = jnp.round(low * jnp.where(lane < MEAN, factor, 0.0)).astype(jnp.int32)
    low = jnp.where(lane == MEAN, ((mean & 0xFFFF) ^ 0x8000) - 0x8000, low)
    low = jnp.where(lane == EXP_W, step_w.astype(jnp.int32), low)
    low = jnp.where(lane == EXP_F, step_f.astype(jnp.int32), low)
    high = jnp.round(high * jnp.where(lane < MEAN, factor, 0.0)).astype(jnp.int32)
    high = jnp.where(lane == MEAN, mean >> 16, high)
    both = jnp.concatenate([low, high], axis=0)
    digits = jnp.concatenate([both >> 8, both & 255], axis=0).astype(jnp.float32).astype(jnp.bfloat16)

    owner = owner_ref[...]
    local = owner & (NODE_DEV - 1)
    target = owner // (N_HARM * NODE_DEV)
    first, second = target[0:1], target[1:2]
    square = (pairs, pairs)
    row_first = jnp.broadcast_to(first, square)
    row_second = jnp.broadcast_to(second, square)
    column_first = row_first.T
    column_second = row_second.T
    before = lax.broadcasted_iota(jnp.int32, square, 0) < lax.broadcasted_iota(jnp.int32, square, 1)
    count_first = jnp.where(before & (column_first == row_first), 1, 0)
    count_second = jnp.where(column_first == row_second, 1, 0) + jnp.where(
        before & (column_second == row_second), 1, 0
    )
    place_first = jnp.sum(count_first, axis=0, keepdims=True)
    place_second = jnp.sum(count_second, axis=0, keepdims=True)

    def slot_of(dest, place):
        part = {
            "x": dest // (SIZES["z"] * SIZES["c"]),
            "z": dest // SIZES["c"] % SIZES["z"],
            "c": dest % SIZES["c"],
        }
        return index_along(FIRST, part) * GROUP + index_along(REST, part) * CAP + place

    slot = lax.broadcasted_iota(jnp.int32, (SLOTS, pairs), 0)
    hit_first = slot == slot_of(first, place_first)
    hit_second = slot == slot_of(second, place_second)
    node = jnp.where(hit_first, local[0:1] + 1, 0) + jnp.where(hit_second, local[1:2] + 1, 0)
    node = jnp.sum(node, axis=1, keepdims=True) - 1
    pick = jnp.where(hit_first | hit_second, 1.0, 0.0).astype(jnp.bfloat16)
    sent = lax.dot_general(
        pick, digits, (((1,), (1,)), ((), ())), preferred_element_type=jnp.float32
    )
    value_low = (sent[:, :LANES] * 256.0 + sent[:, 2 * LANES : 3 * LANES]).astype(jnp.int32)
    value_high = (sent[:, LANES : 2 * LANES] * 256.0 + sent[:, 3 * LANES :]).astype(jnp.int32)
    words = (value_high << 16) | (value_low & 0xFFFF)
    word_lane = lax.broadcasted_iota(jnp.int32, (SLOTS, LANES), 1)
    out_ref[...] = jnp.where(word_lane == NODE, node, words)


def decode(words, mean_unit):
    lane = lax.broadcasted_iota(jnp.int32, words.shape, words.ndim - 1)
    low = ((words & 0xFFFF) ^ 0x8000) - 0x8000
    high = words >> 16
    step = jnp.where(
        lane < W_LANES, ((words[:, EXP_W : EXP_W + 1] & 0xFFFF) ^ 0x8000) - 0x8000,
        ((words[:, EXP_F : EXP_F + 1] & 0xFFFF) ^ 0x8000) - 0x8000,
    )
    scale = jnp.exp2(step.astype(jnp.float32) * (1.0 / STEPS)) * (1.0 / TOP)
    scale = jnp.where(lane < MEAN, scale, jnp.where(lane == MEAN, 1.0 / mean_unit, 0.0))
    low = jnp.where(lane == MEAN, words, low).astype(jnp.float32) * scale
    high = high.astype(jnp.float32) * jnp.where(lane < MEAN, scale, 0.0)
    return jnp.concatenate([low, high], axis=1)


def split_terms(values, count):
    terms = []
    for _ in range(count):
        term = values.astype(jnp.bfloat16)
        terms.append(term)
        values = values - term.astype(jnp.float32)
    return terms


def merge_kernel(words_ref, out_ref):
    words = words_ref[...]
    values = decode(words, MEAN_PAIR)
    rows = N_REST * NODE_DEV
    place = lax.broadcasted_iota(jnp.int32, (SLOTS, 1), 0) % GROUP // CAP
    node = words[:, NODE : NODE + 1]
    node = jnp.where(node >= 0, node + place * NODE_DEV, -1)
    owner = lax.broadcasted_iota(jnp.int32, (SLOTS, rows), 1) == node
    owner = jnp.where(owner, 1.0, 0.0).astype(jnp.bfloat16)
    terms = jnp.concatenate(split_terms(values, 3), axis=1)
    total = lax.dot_general(
        owner, terms, (((0,), (0,)), ((), ())), preferred_element_type=jnp.float32
    )
    low = total[:, :LANES] + (total[:, 2 * LANES : 3 * LANES] + total[:, 4 * LANES : 5 * LANES])
    high = total[:, LANES : 2 * LANES] + (total[:, 3 * LANES : 4 * LANES] + total[:, 5 * LANES :])
    size = jnp.maximum(jnp.abs(low), jnp.abs(high))
    lane = lax.broadcasted_iota(jnp.int32, size.shape, 1)
    step_w = scale_step(jnp.max(jnp.where(lane < W_LANES, size, 0.0), axis=1, keepdims=True))
    step_f = scale_step(
        jnp.max(jnp.where((lane >= W_LANES) & (lane < MEAN), size, 0.0), axis=1, keepdims=True)
    )
    factor = jnp.exp2(jnp.where(lane < W_LANES, step_w, step_f) * (-1.0 / STEPS)) * TOP
    factor = jnp.where(lane < MEAN, factor, 0.0)
    words = (jnp.round(high * factor).astype(jnp.int32) << 16) | (
        jnp.round(low * factor).astype(jnp.int32) & 0xFFFF
    )
    words = jnp.where(lane == MEAN, jnp.round(low * MEAN_NODE).astype(jnp.int32), words)
    words = jnp.where(lane == EXP_W, step_w.astype(jnp.int32), words)
    words = jnp.where(lane == EXP_F, step_f.astype(jnp.int32), words)
    for part in range(N_REST):
        for harm in range(N_HARM):
            start = (part * N_HARM + harm) * NODE_DEV
            out_ref[start : start + NODE_DEV] = words[part * NODE_DEV : (part + 1) * NODE_DEV]


def expand_kernel(words_ref, table_ref, out_ref, held_ref, sem):
    harm = lax.axis_index("h")
    copy = pltpu.make_async_copy(table_ref.at[harm], held_ref, sem)
    copy.start()
    nodes = N_HARM * NODE_DEV
    values = decode(words_ref[:nodes], MEAN_NODE)
    for part in range(1, N_REST):
        values += decode(words_ref[part * nodes : (part + 1) * nodes], MEAN_NODE)
    terms = jnp.concatenate(split_terms(values, 2), axis=0)
    copy.wait()
    blocks = lax.dot_general(
        held_ref[...], terms, (((1,), (1,)), ((), ())), preferred_element_type=jnp.float32
    )
    blocks = (blocks[:, :nodes] + blocks[:, nodes:]).reshape(PER, PAD, nodes)
    out_ref[...] = blocks[:, :COEFS].astype(jnp.bfloat16)


def on_device(stick, stiffness, slip_tangent, contact_force, owner_node, live_pairs):
    pairs = stick.shape[1]
    vmem = pl.BlockSpec(memory_space=pltpu.VMEM)
    params = pltpu.CompilerParams(vmem_limit_bytes=32 * 1024 * 1024)
    slots = pl.pallas_call(
        send_kernel,
        out_shape=jax.ShapeDtypeStruct((SLOTS, LANES), jnp.int32),
        in_specs=[pl.BlockSpec(memory_space=pltpu.SMEM)] + [vmem] * 6,
        out_specs=vmem,
        compiler_params=params,
    )(
        live_pairs,
        stick,
        stiffness.reshape(1, pairs),
        slip_tangent,
        contact_force,
        owner_node,
        jnp.asarray(analysis_table()),
    )
    slots = lax.all_to_all(slots.reshape(N_FIRST, GROUP, LANES), FIRST, 0, 0, tiled=True)
    sums = pl.pallas_call(
        merge_kernel,
        out_shape=jax.ShapeDtypeStruct((N_REST * N_HARM * NODE_DEV, LANES), jnp.int32),
        in_specs=[vmem],
        out_specs=vmem,
        compiler_params=params,
    )(slots.reshape(SLOTS, LANES))
    sums = lax.all_to_all(
        sums.reshape(N_REST * N_HARM, NODE_DEV, LANES), REST + ("h",), 0, 0, tiled=True
    )
    blocks = pl.pallas_call(
        expand_kernel,
        out_shape=jax.ShapeDtypeStruct((PER, COEFS, N_HARM * NODE_DEV), jnp.bfloat16),
        in_specs=[vmem, pl.BlockSpec(memory_space=pl.ANY)],
        out_specs=vmem,
        scratch_shapes=[pltpu.VMEM((T_ROWS, 2 * LANES), jnp.bfloat16), pltpu.SemaphoreType.DMA],
        compiler_params=params,
    )(sums.reshape(N_REST * N_HARM * NODE_DEV, LANES), jnp.asarray(synthesis_table()))
    return jnp.transpose(blocks, (1, 0, 2))


def solution(mesh):
    fine = Mesh(mesh.devices.reshape(tuple(SIZES.values())), tuple(SIZES))
    every = ("x", "z", "c", "h")
    return jax.shard_map(
        on_device,
        mesh=fine,
        in_specs=(P(None, every), P(every), P(None, every), P(None, every), P(None, every), P(every)),
        out_specs=P(None, "h", ("x", "z", "c")),
        check_vma=False,
    )
```

time: 526 us -> 61.4 us (0.12); the launches traced: 520 us -> 61.1 us
  waiting for transfers between devices: 406 us -> 0 us
  blocking collectives: 11.1 us -> 50.3 us
  starting transfers between devices: 37 us -> 0 us
  local copies, waits for them, and re-layouts: 37.4 us -> 6.79 us
  other arithmetic: 15 us -> 0 us
  matrix products: 12.4 us -> 0 us
    all_to_all x2 -> x0, waiting for transfers between devices: 406 us -> none  [the longest x1 406 us: on_device(): lax.all_to_all(outgoing, 'pair', split_axis=1, concat_axis=1, tiled=True)]
    all_to_all x1 -> x2, blocking collectives: 11.1 us -> 50.3 us  [the longest x1 38 us: on_device(): lax.all_to_all(slots.reshape(N_FIRST, GROUP, LANES), FIRST, 0, 0, tiled=T...]
    all_to_all x2 -> x0, starting transfers between devices: 37 us -> none  [the longest x1 20.4 us: on_device(): lax.all_to_all(node_id, 'pair', split_axis=1, concat_axis=1, tiled=True)]
    gather x3 -> x0, local copies, waits for them, and re-layouts: 17.7 us -> none  [the longest x2 14.9 us: on_device(): outgoing = jnp.take(pair_block, column, axis=1)]
    select_n x7 -> x0, other arithmetic: 12.9 us -> none  [the longest x1 10.4 us: on_device(): outgoing = jnp.take(pair_block, column, axis=1)]
    all_to_all x5 -> x0, local copies, waits for them, and re-layouts: 12.6 us -> none  [the longest x1 10.2 us: on_device(): lax.all_to_all(outgoing, 'pair', split_axis=1, concat_axis=1, tiled=True)]
    dot_general x3 -> x0, matrix products: 12.4 us -> none  [the longest x1 5.71 us: on_device(): summed = jnp.dot(arrived, owner_table(arrived_ids), precision=precise)]
    unnamed x1 -> x14, local copies, waits for them, and re-layouts: 0.01 us -> 6.79 us
  transfers between devices with their start and end apart: 2 -> 0, of which waited for: 1 -> 0; matrix products, arithmetic and copies ran while one was open for 7% -> 0% of each run, Pallas kernels for 0% -> 0%
where the time goes in v1:
time: 61.4 us; the launch traced here: 61.1 us
  blocking collectives  50.3 us (82%)
  local copies, waits for them, and re-layouts  6.79 us (11%)
  Pallas kernels  3.32 us (5%)
  between operations  0.68 us (1%)
    all_to_all x1, blocking collectives, on_device(): lax.all_to_all(slots.reshape(N_FIRST, GROUP, LANES), FIRST, 0, 0, tiled=T...  38 us
    all_to_all x1, blocking collectives, on_device(): lax.all_to_all(sums.reshape(N_REST * N_HARM, NODE_DEV, LANES), REST + ('h...  12.3 us
    unnamed x14, local copies, waits for them, and re-layouts  6.79 us
    pallas_call x1, Pallas kernels, on_device(): pl.pallas_call(expand_kernel, out_shape=jax.ShapeDtypeStruct((PER, COEFS,...  1.42 us

profile of v1, /device:TPU:1, one launch (start us, length us, event | category | flops | bytes accessed | tf_op | source)
XLA Modules:
  0.0 61.1 jit_solution(1394540921873680375)
XLA Ops:
  0.7 0.0 copy-start.1
  0.7 1.0 %copy-done.1 = f32[256,512]{1,0:T(8,128)S(1)} copy-done((f32[256,512]{1,0:T(8,128)S(1)}, f32[256,512]{1,0:T(8,128)}, u32[]{:S(2)}) %copy-start.1) | copy-done | bytes 524312
  1.7 0.0 copy-start.2
  1.7 0.9 %copy-done.2 = s32[256,128]{1,0:T(8,128)S(1)} copy-done((s32[256,128]{1,0:T(8,128)S(1)}, s32[256,128]{1,0:T(8,128)}, u32[]{:S(2)}) %copy-start.2) | copy-done | bytes 131096
  2.6 0.0 copy-start.3
  2.6 0.9 %copy-done.3 = f32[256,128]{1,0:T(8,128)S(1)} copy-done((f32[256,128]{1,0:T(8,128)S(1)}, f32[256,128]{1,0:T(8,128)}, u32[]{:S(2)}) %copy-start.3) | copy-done | bytes 131096
  3.5 0.0 copy-start.4
  3.5 0.9 %copy-done.4 = f32[256,128]{1,0:T(8,128)S(1)} copy-done((f32[256,128]{1,0:T(8,128)S(1)}, f32[256,128]{1,0:T(8,128)}, u32[]{:S(2)}) %copy-start.4) | copy-done | bytes 131096
  4.4 0.0 copy-start.5
  4.4 0.7 %copy-done.5 = s32[2,128]{1,0:T(2,128)S(1)} copy-done((s32[2,128]{1,0:T(2,128)S(1)}, s32[2,128]{1,0:T(2,128)}, u32[]{:S(2)}) %copy-start.5) | copy-done | bytes 1048
  5.1 0.0 copy-start.6
  5.1 0.7 %copy-done.6 = f32[128]{0:T(128)S(1)} copy-done((f32[128]{0:T(128)S(1)}, f32[128]{0:T(128)}, u32[]{:S(2)}) %copy-start.6) | copy-done | bytes 536
  5.7 1.2 %shard_map.82 = s32[512,128]{1,0:T(8,128)S(1)} custom-call(s32[1]{0:T(128)S(6)} %copy.9.live_ref, s32[256,128]{1,0:T(8,128)S(1)} %copy-done.2, f32[1,128]{1,0:T(1,128)S(1)} %bitcast.10, f32[256,128]{1,0:T(8,128)S(1)} %copy-done.3, f32[256,128]{1,0:T(8,128)S(1)} %copy-done.4, s32[2,128]{1,0:T(2,128)S(1)} %copy-done.5, f32[256,512]{1,0:T(8,128)S(1)} %copy-done.1), custom_call_target="tpu_custom_call" | custom-call | tf_op jit(solution)/shard_map/pallas_call | solution.py:258
  6.9 38.0 %all_to_all.10 = s32[64,8,128]{2,1,0:T(8,128)S(1)} all-to-all(s32[64,8,128]{2,1,0:T(8,128)S(1)} %bitcast.7), channel_id=1, replica_groups=mesh['x'=4,'z'=16,'c'=2,'h'=4] {'x','z'}, dimensions={0} | all-to-all | bytes 524288 | tf_op jit(solution)/shard_map/all_to_all | solution.py:273
  44.9 0.7 %shard_map.83 = s32[256,128]{1,0:T(8,128)S(1)} custom-call(s32[512,128]{1,0:T(8,128)S(1)} %bitcast.6), custom_call_target="tpu_custom_call" | custom-call | tf_op jit(solution)/shard_map/pallas_call | solution.py:274
  45.6 12.3 %all_to_all.11 = s32[8,32,128]{2,1,0:T(8,128)S(1)} all-to-all(s32[8,32,128]{2,1,0:T(8,128)S(1)} %bitcast.9), channel_id=1, replica_groups=mesh['x'=4,'z'=16,'c'=2,'h'=4] {'c','h'}, dimensions={0} | all-to-all | bytes 262144 | tf_op jit(solution)/shard_map/all_to_all | solution.py:281
  57.9 0.0 copy-start
  57.9 1.7 %copy-done = bf16[4,1224,256]{2,1,0:T(8,128)(2,1)S(1)} copy-done((bf16[4,1224,256]{2,1,0:T(8,128)(2,1)S(1)}, bf16[4,1224,256]{2,1,0:T(8,128)(2,1)}, u32[]{:S(2)}) %copy-start) | copy-done | bytes 2506776
  59.6 1.4 %shard_map.84 = bf16[17,67,128]{2,1,0:T(8,128)(2,1)} custom-call(s32[256,128]{1,0:T(8,128)S(1)} %bitcast.8, bf16[4,1224,256]{2,1,0:T(8,128)(2,1)S(1)} %copy-done), custom_call_target="tpu_custom_call" | custom-call | tf_op jit(solution)/shard_map/pallas_call | solution.py:284
Async XLA Ops:
  0.7 1.0 %copy-start.1 = (f32[256,512]{1,0:T(8,128)S(1)}, f32[256,512]{1,0:T(8,128)}, u32[]{:S(2)}) copy-start(f32[256,512]{1,0:T(8,128)} %constant.4.clone.table_ref) | copy-start | bytes 1572868
  1.7 0.9 %copy-start.2 = (s32[256,128]{1,0:T(8,128)S(1)}, s32[256,128]{1,0:T(8,128)}, u32[]{:S(2)}) copy-start(s32[256,128]{1,0:T(8,128)} %stick_ref.1) | copy-start | bytes 393220
  2.6 0.9 %copy-start.3 = (f32[256,128]{1,0:T(8,128)S(1)}, f32[256,128]{1,0:T(8,128)}, u32[]{:S(2)}) copy-start(f32[256,128]{1,0:T(8,128)} %slip_ref.1) | copy-start | bytes 393220
  3.5 0.9 %copy-start.4 = (f32[256,128]{1,0:T(8,128)S(1)}, f32[256,128]{1,0:T(8,128)}, u32[]{:S(2)}) copy-start(f32[256,128]{1,0:T(8,128)} %force_ref.1) | copy-start | bytes 393220
  4.4 0.7 %copy-start.5 = (s32[2,128]{1,0:T(2,128)S(1)}, s32[2,128]{1,0:T(2,128)}, u32[]{:S(2)}) copy-start(s32[2,128]{1,0:T(2,128)} %owner_ref.1) | copy-start | bytes 3076
  5.1 0.7 %copy-start.6 = (f32[128]{0:T(128)S(1)}, f32[128]{0:T(128)}, u32[]{:S(2)}) copy-start(f32[128]{0:T(128)} %param.9) | copy-start | bytes 1540
  57.9 1.7 %copy-start = (bf16[4,1224,256]{2,1,0:T(8,128)(2,1)S(1)}, bf16[4,1224,256]{2,1,0:T(8,128)(2,1)}, u32[]{:S(2)}) copy-start(bf16[4,1224,256]{2,1,0:T(8,128)(2,1)} %constant.5.clone.table_ref) | copy-start | bytes 7520260

commit v2 on v1

--- a/solution.py
+++ b/solution.py
@@ -16,7 +16,7 @@
 NODE_DEV = 32
 CAP = 3
 SIZES = {"x": 4, "z": 16, "c": 2, "h": 4}
-FIRST = ("x", "z")
+FIRST = ("z",)
 REST = tuple(axis for axis in ("x", "z", "c") if axis not in FIRST)
 N_FIRST = math.prod(SIZES[axis] for axis in FIRST)
 N_REST = math.prod(SIZES[axis] for axis in REST)
@@ -104,36 +104,27 @@
     return jnp.ceil(jnp.log2(jnp.maximum(largest, 1e-30)) * STEPS + 0.01)
 
 
-def send_kernel(live_ref, stick_ref, stiff_ref, slip_ref, force_ref, owner_ref, table_ref, out_ref):
+def send_kernel(
+    live_ref, stick_hbm, stiff_hbm, slip_hbm, force_hbm, owner_hbm, table_hbm, out_ref,
+    stick_ref, stiff_ref, slip_ref, force_ref, owner_ref, table_ref, sems,
+):
+    copies = [
+        pltpu.make_async_copy(source, held, sems.at[n])
+        for n, (source, held) in enumerate(
+            (
+                (owner_hbm, owner_ref),
+                (stiff_hbm, stiff_ref),
+                (stick_hbm, stick_ref),
+                (slip_hbm, slip_ref),
+                (force_hbm, force_ref),
+                (table_hbm, table_ref),
+            )
+        )
+    ]
+    for copy in copies:
+        copy.start()
     pairs = stick_ref.shape[1]
-    live = (lax.broadcasted_iota(jnp.int32, (1, pairs), 1) < live_ref[0]).astype(jnp.float32)
-    stick = stick_ref[...].astype(jnp.float32)
-    weights = (stiff_ref[...] * live) * (stick + (1.0 - stick) * slip_ref[...])
-    forces = force_ref[...] * live
-    sums = jnp.dot(
-        table_ref[...],
-        jnp.concatenate([weights, forces], axis=0),
-        precision=lax.Precision.HIGHEST,
-        preferred_element_type=jnp.float32,
-    )
-    low, high = sums[:LANES], sums[LANES:]
-    size = jnp.maximum(jnp.abs(low), jnp.abs(high))
-    step_w = scale_step(jnp.max(size[:W_LANES], axis=0, keepdims=True))
-    step_f = scale_step(jnp.max(size[W_LANES:MEAN], axis=0, keepdims=True))
-    lane = lax.broadcasted_iota(jnp.int32, (LANES, pairs), 0)
-    factor = jnp.where(
-        lane < W_LANES, jnp.exp2(step_w * (-1.0 / STEPS)) * TOP, jnp.exp2(step_f * (-1.0 / STEPS)) * TOP
-    )
-    mean = jnp.round(sums[MEAN : MEAN + 1] * MEAN_PAIR).astype(jnp.int32)
-    low = jnp.round(low * jnp.where(lane < MEAN, factor, 0.0)).astype(jnp.int32)
-    low = jnp.where(lane == MEAN, ((mean & 0xFFFF) ^ 0x8000) - 0x8000, low)
-    low = jnp.where(lane == EXP_W, step_w.astype(jnp.int32), low)
-    low = jnp.where(lane == EXP_F, step_f.astype(jnp.int32), low)
-    high = jnp.round(high * jnp.where(lane < MEAN, factor, 0.0)).astype(jnp.int32)
-    high = jnp.where(lane == MEAN, mean >> 16, high)
-    both = jnp.concatenate([low, high], axis=0)
-    digits = jnp.concatenate([both >> 8, both & 255], axis=0).astype(jnp.float32).astype(jnp.bfloat16)
-
+    copies[0].wait()
     owner = owner_ref[...]
     local = owner & (NODE_DEV - 1)
     target = owner // (N_HARM * NODE_DEV)
@@ -165,6 +156,35 @@
     node = jnp.where(hit_first, local[0:1] + 1, 0) + jnp.where(hit_second, local[1:2] + 1, 0)
     node = jnp.sum(node, axis=1, keepdims=True) - 1
     pick = jnp.where(hit_first | hit_second, 1.0, 0.0).astype(jnp.bfloat16)
+    for copy in copies[1:]:
+        copy.wait()
+    live = (lax.broadcasted_iota(jnp.int32, (1, pairs), 1) < live_ref[0]).astype(jnp.float32)
+    stick = stick_ref[...].astype(jnp.float32)
+    weights = (stiff_ref[...] * live) * (stick + (1.0 - stick) * slip_ref[...])
+    forces = force_ref[...] * live
+    sums = jnp.dot(
+        table_ref[...],
+        jnp.concatenate([weights, forces], axis=0),
+        precision=lax.Precision.HIGHEST,
+        preferred_element_type=jnp.float32,
+    )
+    low, high = sums[:LANES], sums[LANES:]
+    size = jnp.maximum(jnp.abs(low), jnp.abs(high))
+    step_w = scale_step(jnp.max(size[:W_LANES], axis=0, keepdims=True))
+    step_f = scale_step(jnp.max(size[W_LANES:MEAN], axis=0, keepdims=True))
+    lane = lax.broadcasted_iota(jnp.int32, (LANES, pairs), 0)
+    factor = jnp.where(
+        lane < W_LANES, jnp.exp2(step_w * (-1.0 / STEPS)) * TOP, jnp.exp2(step_f * (-1.0 / STEPS)) * TOP
+    )
+    mean = jnp.round(sums[MEAN : MEAN + 1] * MEAN_PAIR).astype(jnp.int32)
+    low = jnp.round(low * jnp.where(lane < MEAN, factor, 0.0)).astype(jnp.int32)
+    low = jnp.where(lane == MEAN, ((mean & 0xFFFF) ^ 0x8000) - 0x8000, low)
+    low = jnp.where(lane == EXP_W, step_w.astype(jnp.int32), low)
+    low = jnp.where(lane == EXP_F, step_f.astype(jnp.int32), low)
+    high = jnp.round(high * jnp.where(lane < MEAN, factor, 0.0)).astype(jnp.int32)
+    high = jnp.where(lane == MEAN, mean >> 16, high)
+    both = jnp.concatenate([low, high], axis=0)
+    digits = jnp.concatenate([both >> 8, both & 255], axis=0).astype(jnp.float32).astype(jnp.bfloat16)
     sent = lax.dot_general(
         pick, digits, (((1,), (1,)), ((), ())), preferred_element_type=jnp.float32
     )
@@ -251,24 +271,38 @@
     out_ref[...] = blocks[:, :COEFS].astype(jnp.bfloat16)
 
 
+def in_hbm(array):
+    return pltpu.with_memory_space_constraint(array, pltpu.HBM)
+
+
 def on_device(stick, stiffness, slip_tangent, contact_force, owner_node, live_pairs):
     pairs = stick.shape[1]
     vmem = pl.BlockSpec(memory_space=pltpu.VMEM)
+    hbm = pl.BlockSpec(memory_space=pltpu.HBM)
     params = pltpu.CompilerParams(vmem_limit_bytes=32 * 1024 * 1024)
     slots = pl.pallas_call(
         send_kernel,
         out_shape=jax.ShapeDtypeStruct((SLOTS, LANES), jnp.int32),
-        in_specs=[pl.BlockSpec(memory_space=pltpu.SMEM)] + [vmem] * 6,
+        in_specs=[pl.BlockSpec(memory_space=pltpu.SMEM)] + [hbm] * 6,
         out_specs=vmem,
+        scratch_shapes=[
+            pltpu.VMEM((SAMPLES, pairs), jnp.int32),
+            pltpu.VMEM((1, pairs), jnp.float32),
+            pltpu.VMEM((SAMPLES, pairs), jnp.float32),
+            pltpu.VMEM((SAMPLES, pairs), jnp.float32),
+            pltpu.VMEM((2, pairs), jnp.int32),
+            pltpu.VMEM((2 * LANES, 2 * SAMPLES), jnp.float32),
+            pltpu.SemaphoreType.DMA((6,)),
+        ],
         compiler_params=params,
     )(
         live_pairs,
-        stick,
-        stiffness.reshape(1, pairs),
-        slip_tangent,
-        contact_force,
-        owner_node,
-        jnp.asarray(analysis_table()),
+        in_hbm(stick),
+        in_hbm(stiffness.reshape(1, pairs)),
+        in_hbm(slip_tangent),
+        in_hbm(contact_force),
+        in_hbm(owner_node),
+        in_hbm(jnp.asarray(analysis_table())),
     )
     slots = lax.all_to_all(slots.reshape(N_FIRST, GROUP, LANES), FIRST, 0, 0, tiled=True)
     sums = pl.pallas_call(
@@ -284,11 +318,11 @@
     blocks = pl.pallas_call(
         expand_kernel,
         out_shape=jax.ShapeDtypeStruct((PER, COEFS, N_HARM * NODE_DEV), jnp.bfloat16),
-        in_specs=[vmem, pl.BlockSpec(memory_space=pl.ANY)],
+        in_specs=[vmem, hbm],
         out_specs=vmem,
         scratch_shapes=[pltpu.VMEM((T_ROWS, 2 * LANES), jnp.bfloat16), pltpu.SemaphoreType.DMA],
         compiler_params=params,
-    )(sums.reshape(N_REST * N_HARM * NODE_DEV, LANES), jnp.asarray(synthesis_table()))
+    )(sums.reshape(N_REST * N_HARM * NODE_DEV, LANES), in_hbm(jnp.asarray(synthesis_table())))
     return jnp.transpose(blocks, (1, 0, 2))
 
 

time: 61.4 us -> 57.3 us (0.933)
  local copies, waits for them, and re-layouts: 6.79 us -> 0 us
  Pallas kernels: 3.32 us -> 5.56 us
    all_to_all x1, blocking collectives: 12.3 us -> 22.8 us  [on_device(): lax.all_to_all(sums.reshape(N_REST * N_HARM, NODE_DEV, LANES), REST + ('h...]
    all_to_all x1, blocking collectives: 38 us -> 28.1 us  [on_device(): lax.all_to_all(slots.reshape(N_FIRST, GROUP, LANES), FIRST, 0, 0, tiled=T...]
    unnamed x14 -> x0, local copies, waits for them, and re-layouts: 6.79 us -> none
    pallas_call x1, Pallas kernels: 1.17 us -> 2.39 us  [on_device(): pl.pallas_call(send_kernel, out_shape=jax.ShapeDtypeStruct((SLOTS, LANES)...]
    pallas_call x1, Pallas kernels: 1.42 us -> 2.19 us  [on_device(): pl.pallas_call(expand_kernel, out_shape=jax.ShapeDtypeStruct((PER, COEFS,...]
where the time goes in v2:
time: 57.3 us; the launch traced here: 57.1 us
  blocking collectives  50.9 us (89%)
  Pallas kernels  5.56 us (10%)
  between operations  0.67 us (1%)
    all_to_all x1, blocking collectives, on_device(): lax.all_to_all(slots.reshape(N_FIRST, GROUP, LANES), FIRST, 0, 0, tiled=T...  28.1 us
    all_to_all x1, blocking collectives, on_device(): lax.all_to_all(sums.reshape(N_REST * N_HARM, NODE_DEV, LANES), REST + ('h...  22.8 us
    pallas_call x1, Pallas kernels, on_device(): pl.pallas_call(send_kernel, out_shape=jax.ShapeDtypeStruct((SLOTS, LANES)...  2.39 us
    pallas_call x1, Pallas kernels, on_device(): pl.pallas_call(expand_kernel, out_shape=jax.ShapeDtypeStruct((PER, COEFS,...  2.19 us

profile of v2, /device:TPU:1, one launch (start us, length us, event | category | flops | bytes accessed | tf_op | source)
XLA Modules:
  0.0 57.1 jit_solution(6601510710746843178)
XLA Ops:
  0.7 2.4 %shard_map.82 = s32[384,128]{1,0:T(8,128)S(1)} custom-call(s32[1]{0:T(128)S(6)} %copy.9.live_ref, s32[256,128]{1,0:T(8,128)} %stick_hbm.1, f32[1,128]{1,0:T(1,128)} %bitcast.10, f32[256,128]{1,0:T(8,128)} %slip_hbm.1, f32[256,128]{1,0:T(8,128)} %force_hbm.1, s32[2,128]{1,0:T(2,128)} %owner_hbm.1, f32[256,512]{1,0:T(8,128)} %constant.4.clone.table_hbm), custom_call_target="tpu_custom_call" | custom-call | tf_op jit(solution)/shard_map/pallas_call | solution.py:283
  3.1 28.1 %all_to_all.10 = s32[16,24,128]{2,1,0:T(8,128)S(1)} all-to-all(s32[16,24,128]{2,1,0:T(8,128)S(1)} %bitcast.9), channel_id=1, replica_groups=mesh['x'=4,'z'=16,'c'=2,'h'=4] {'z'}, dimensions={0} | all-to-all | bytes 393216 | tf_op jit(solution)/shard_map/all_to_all | solution.py:307
  31.2 1.0 %shard_map.83 = s32[1024,128]{1,0:T(8,128)S(1)} custom-call(s32[384,128]{1,0:T(8,128)S(1)} %bitcast.8), custom_call_target="tpu_custom_call" | custom-call | tf_op jit(solution)/shard_map/pallas_call | solution.py:308
  32.1 22.8 %all_to_all.11 = s32[32,32,128]{2,1,0:T(8,128)S(1)} all-to-all(s32[32,32,128]{2,1,0:T(8,128)S(1)} %bitcast.6), channel_id=1, replica_groups=mesh['x'=4,'z'=16,'c'=2,'h'=4] {'x','c','h'}, dimensions={0} | all-to-all | bytes 1048576 | tf_op jit(solution)/shard_map/all_to_all | solution.py:315
  54.9 2.2 %shard_map.84 = bf16[17,67,128]{2,1,0:T(8,128)(2,1)} custom-call(s32[1024,128]{1,0:T(8,128)S(1)} %bitcast.7, bf16[4,1224,256]{2,1,0:T(8,128)(2,1)} %constant.5.clone.table_ref), custom_call_target="tpu_custom_call" | custom-call | tf_op jit(solution)/shard_map/pallas_call | solution.py:318

commit v3 on v2

--- a/solution.py
+++ b/solution.py
@@ -16,12 +16,12 @@
 NODE_DEV = 32
 CAP = 3
 SIZES = {"x": 4, "z": 16, "c": 2, "h": 4}
-FIRST = ("z",)
+FIRST = ("x", "z")
 REST = tuple(axis for axis in ("x", "z", "c") if axis not in FIRST)
 N_FIRST = math.prod(SIZES[axis] for axis in FIRST)
 N_REST = math.prod(SIZES[axis] for axis in REST)
 N_HARM = SIZES["h"]
-GROUP = -(-N_REST * CAP // 8) * 8
+GROUP = N_REST * CAP
 SLOTS = N_FIRST * GROUP
 
 LANES = 128
@@ -304,7 +304,7 @@
         in_hbm(owner_node),
         in_hbm(jnp.asarray(analysis_table())),
     )
-    slots = lax.all_to_all(slots.reshape(N_FIRST, GROUP, LANES), FIRST, 0, 0, tiled=True)
+    slots = lax.all_to_all(slots.reshape(N_FIRST, 1, GROUP * LANES), FIRST, 0, 0, tiled=True)
     sums = pl.pallas_call(
         merge_kernel,
         out_shape=jax.ShapeDtypeStruct((N_REST * N_HARM * NODE_DEV, LANES), jnp.int32),

time: 57.3 us -> 53.7 us (0.937)
  blocking collectives: 50.9 us -> 47.5 us
    all_to_all x1, blocking collectives: 22.8 us -> 12 us  [on_device(): lax.all_to_all(sums.reshape(N_REST * N_HARM, NODE_DEV, LANES), REST + ('h...]
    all_to_all x1, blocking collectives: 28.1 us -> 35.6 us  [on_device(): lax.all_to_all(slots.reshape(N_FIRST, 1, GROUP * LANES), FIRST, 0, 0, til...]
where the time goes in v3:
time: 53.7 us; the launch traced here: 53.5 us
  blocking collectives  47.5 us (88%)
  Pallas kernels  5.29 us (10%)
  between operations  0.67 us (1%)
    all_to_all x1, blocking collectives, on_device(): lax.all_to_all(slots.reshape(N_FIRST, 1, GROUP * LANES), FIRST, 0, 0, til...  35.6 us
    all_to_all x1, blocking collectives, on_device(): lax.all_to_all(sums.reshape(N_REST * N_HARM, NODE_DEV, LANES), REST + ('h...  12 us
    pallas_call x1, Pallas kernels, on_device(): pl.pallas_call(send_kernel, out_shape=jax.ShapeDtypeStruct((SLOTS, LANES)...  2.39 us
    pallas_call x1, Pallas kernels, on_device(): pl.pallas_call(expand_kernel, out_shape=jax.ShapeDtypeStruct((PER, COEFS,...  2.18 us

profile of v3, /device:TPU:1, one launch (start us, length us, event | category | flops | bytes accessed | tf_op | source)
XLA Modules:
  0.0 53.5 jit_solution(9808190988272458797)
XLA Ops:
  0.7 2.4 %shard_map.82 = s32[384,128]{1,0:T(8,128)S(1)} custom-call(s32[1]{0:T(128)S(6)} %copy.10.live_ref, s32[256,128]{1,0:T(8,128)} %stick_hbm.1, f32[1,128]{1,0:T(1,128)} %bitcast.10, f32[256,128]{1,0:T(8,128)} %slip_hbm.1, f32[256,128]{1,0:T(8,128)} %force_hbm.1, s32[2,128]{1,0:T(2,128)} %owner_hbm.1, f32[256,512]{1,0:T(8,128)} %constant.4.clone.table_hbm), custom_call_target="tpu_custom_call" | custom-call | tf_op jit(solution)/shard_map/pallas_call | solution.py:283
  3.1 35.6 %all_to_all.10 = s32[64,1,768]{2,1,0:T(1,128)S(1)} all-to-all(s32[64,1,768]{2,1,0:T(1,128)S(1)} %bitcast.7), channel_id=1, replica_groups=mesh['x'=4,'z'=16,'c'=2,'h'=4] {'x','z'}, dimensions={0} | all-to-all | bytes 393216 | tf_op jit(solution)/shard_map/all_to_all | solution.py:307
  38.6 0.7 %shard_map.83 = s32[256,128]{1,0:T(8,128)S(1)} custom-call(s32[384,128]{1,0:T(8,128)S(1)} %bitcast.6), custom_call_target="tpu_custom_call" | custom-call | tf_op jit(solution)/shard_map/pallas_call | solution.py:308
  39.3 12.0 %all_to_all.11 = s32[8,32,128]{2,1,0:T(8,128)S(1)} all-to-all(s32[8,32,128]{2,1,0:T(8,128)S(1)} %bitcast.9), channel_id=1, replica_groups=mesh['x'=4,'z'=16,'c'=2,'h'=4] {'c','h'}, dimensions={0} | all-to-all | bytes 262144 | tf_op jit(solution)/shard_map/all_to_all | solution.py:315
  51.3 2.2 %shard_map.84 = bf16[17,67,128]{2,1,0:T(8,128)(2,1)} custom-call(s32[256,128]{1,0:T(8,128)S(1)} %bitcast.8, bf16[4,1224,256]{2,1,0:T(8,128)(2,1)} %constant.5.clone.table_ref), custom_call_target="tpu_custom_call" | custom-call | tf_op jit(solution)/shard_map/pallas_call | solution.py:318

commit v4 on v3

--- a/solution.py
+++ b/solution.py
@@ -16,7 +16,7 @@
 NODE_DEV = 32
 CAP = 3
 SIZES = {"x": 4, "z": 16, "c": 2, "h": 4}
-FIRST = ("x", "z")
+FIRST = ("x", "z", "c")
 REST = tuple(axis for axis in ("x", "z", "c") if axis not in FIRST)
 N_FIRST = math.prod(SIZES[axis] for axis in FIRST)
 N_REST = math.prod(SIZES[axis] for axis in REST)

time: 53.7 us -> 55.6 us (1.035)
  the two profiles are of different devices: /device:TPU:1 before, /device:TPU:8 now
where the time goes in v4:
time: 55.6 us; the launch traced here: 55.4 us
  blocking collectives  49.4 us (89%)
  Pallas kernels  5.28 us (9%)
  between operations  0.67 us (1%)
    all_to_all x1, blocking collectives, on_device(): lax.all_to_all(slots.reshape(N_FIRST, 1, GROUP * LANES), FIRST, 0, 0, til...  40.6 us
    all_to_all x1, blocking collectives, on_device(): lax.all_to_all(sums.reshape(N_REST * N_HARM, NODE_DEV, LANES), REST + ('h...  8.88 us
    pallas_call x1, Pallas kernels, on_device(): pl.pallas_call(send_kernel, out_shape=jax.ShapeDtypeStruct((SLOTS, LANES)...  2.39 us
    pallas_call x1, Pallas kernels, on_device(): pl.pallas_call(expand_kernel, out_shape=jax.ShapeDtypeStruct((PER, COEFS,...  2.18 us

profile of v4, /device:TPU:8, one launch (start us, length us, event | category | flops | bytes accessed | tf_op | source)
XLA Modules:
  0.0 55.4 jit_solution(11634455431622277607)
XLA Ops:
  0.7 2.4 %shard_map.82 = s32[384,128]{1,0:T(8,128)S(1)} custom-call(s32[1]{0:T(128)S(6)} %copy.10.live_ref, s32[256,128]{1,0:T(8,128)} %stick_hbm.1, f32[1,128]{1,0:T(1,128)} %bitcast.10, f32[256,128]{1,0:T(8,128)} %slip_hbm.1, f32[256,128]{1,0:T(8,128)} %force_hbm.1, s32[2,128]{1,0:T(2,128)} %owner_hbm.1, f32[256,512]{1,0:T(8,128)} %constant.4.clone.table_hbm), custom_call_target="tpu_custom_call" | custom-call | tf_op jit(solution)/shard_map/pallas_call | solution.py:283
  3.1 40.6 %all_to_all.10 = s32[128,1,384]{2,1,0:T(1,128)S(1)} all-to-all(s32[128,1,384]{2,1,0:T(1,128)S(1)} %bitcast.7), channel_id=1, replica_groups=mesh['x'=4,'z'=16,'c'=2,'h'=4] {'x','z','c'}, dimensions={0} | all-to-all | bytes 393216 | tf_op jit(solution)/shard_map/all_to_all | solution.py:307
  43.6 0.7 %shard_map.83 = s32[128,128]{1,0:T(8,128)S(1)} custom-call(s32[384,128]{1,0:T(8,128)S(1)} %bitcast.6), custom_call_target="tpu_custom_call" | custom-call | tf_op jit(solution)/shard_map/pallas_call | solution.py:308
  44.3 8.9 %all_to_all.11 = s32[4,32,128]{2,1,0:T(8,128)S(1)} all-to-all(s32[4,32,128]{2,1,0:T(8,128)S(1)} %bitcast.9), channel_id=1, replica_groups=mesh['x'=4,'z'=16,'c'=2,'h'=4] {'h'}, dimensions={0} | all-to-all | bytes 131072 | tf_op jit(solution)/shard_map/all_to_all | solution.py:315
  53.2 2.2 %shard_map.84 = bf16[17,67,128]{2,1,0:T(8,128)(2,1)} custom-call(s32[128,128]{1,0:T(8,128)S(1)} %bitcast.8, bf16[4,1224,256]{2,1,0:T(8,128)(2,1)} %constant.5.clone.table_ref), custom_call_target="tpu_custom_call" | custom-call | tf_op jit(solution)/shard_map/pallas_call | solution.py:318

commit v5 on v3

--- a/solution.py
+++ b/solution.py
@@ -1,4 +1,3 @@
-import functools
 import math
 
 import jax
@@ -25,9 +24,14 @@
 SLOTS = N_FIRST * GROUP
 
 LANES = 128
-W_LANES = 72
+W_LANES = 66
 F_LOW = 34
-MEAN, EXP_W, EXP_F, NODE = 112, 113, 114, 115
+MEAN, EXP_W, EXP_F, NODE = 100, 101, 102, 103
+RECORD = 104
+F_START = 64
+ROWS = GROUP - 1
+FREE = LANES - RECORD
+W_HIGH = 72
 STEPS = 16.0
 TOP = 32766.0
 MEAN_PAIR = 2.0**21
@@ -45,14 +49,19 @@
     basis[0] = 1.0
     basis[1::2] = cosine[1 : HARMONICS + 1]
     basis[2::2] = sine[1 : HARMONICS + 1]
-    table = np.zeros((2 * LANES, 2 * SAMPLES))
-    top = 2 * HARMONICS
-    table[:top, :SAMPLES] = cosine[1:]
-    table[LANES : LANES + top, :SAMPLES] = sine[1:]
-    table[MEAN, :SAMPLES] = 1.0
-    table[W_LANES : W_LANES + F_LOW, SAMPLES:] = basis[:F_LOW]
-    table[LANES + W_LANES : LANES + W_LANES + COEFS - F_LOW, SAMPLES:] = basis[F_LOW:]
-    return table.astype(np.float32)
+    w_low = np.zeros((RECORD, SAMPLES))
+    w_low[:W_LANES] = cosine[1:]
+    w_low[MEAN] = 1.0
+    w_high = np.zeros((W_HIGH, SAMPLES))
+    w_high[:W_LANES] = sine[1:]
+    f_low = np.zeros((RECORD - F_START, SAMPLES))
+    f_low[W_LANES - F_START : MEAN - F_START] = basis[:F_LOW]
+    f_high = np.zeros_like(f_low)
+    f_high[W_LANES - F_START : W_LANES - F_START + COEFS - F_LOW] = basis[F_LOW:]
+    table = np.concatenate([w_low, w_high, f_low, f_high], axis=0)
+    first = table.astype(jnp.bfloat16)
+    second = (table - first.astype(np.float64)).astype(jnp.bfloat16)
+    return np.concatenate([first, second], axis=0)
 
 
 def synthesis_table():
@@ -104,8 +113,24 @@
     return jnp.ceil(jnp.log2(jnp.maximum(largest, 1e-30)) * STEPS + 0.01)
 
 
+def transform(table_ref, start, stop, samples):
+    total = table_ref.shape[0] // 2
+    first, second = split_terms(samples, 2)
+    large = jnp.dot(
+        table_ref[start:stop],
+        jnp.concatenate([first, second], axis=1),
+        preferred_element_type=jnp.float32,
+    )
+    small = jnp.dot(
+        table_ref[total + start : total + stop], first, preferred_element_type=jnp.float32
+    )
+    pairs = samples.shape[1]
+    return large[:, :pairs] + (large[:, pairs:] + small)
+
+
 def send_kernel(
-    live_ref, stick_hbm, stiff_hbm, slip_hbm, force_hbm, owner_hbm, table_hbm, out_ref,
+    live_ref, stick_hbm, stiff_hbm, slip_hbm, force_hbm, owner_hbm, table_hbm, synthesis_hbm,
+    out_ref, synthesis_ref,
     stick_ref, stiff_ref, slip_ref, force_ref, owner_ref, table_ref, sems,
 ):
     copies = [
@@ -116,8 +141,9 @@
                 (stiff_hbm, stiff_ref),
                 (stick_hbm, stick_ref),
                 (slip_hbm, slip_ref),
+                (table_hbm, table_ref),
                 (force_hbm, force_ref),
-                (table_hbm, table_ref),
+                (synthesis_hbm.at[lax.axis_index("h")], synthesis_ref),
             )
         )
     ]
@@ -148,7 +174,7 @@
             "z": dest // SIZES["c"] % SIZES["z"],
             "c": dest % SIZES["c"],
         }
-        return index_along(FIRST, part) * GROUP + index_along(REST, part) * CAP + place
+        return (index_along(REST, part) * CAP + place) * N_FIRST + index_along(FIRST, part)
 
     slot = lax.broadcasted_iota(jnp.int32, (SLOTS, pairs), 0)
     hit_first = slot == slot_of(first, place_first)
@@ -156,34 +182,43 @@
     node = jnp.where(hit_first, local[0:1] + 1, 0) + jnp.where(hit_second, local[1:2] + 1, 0)
     node = jnp.sum(node, axis=1, keepdims=True) - 1
     pick = jnp.where(hit_first | hit_second, 1.0, 0.0).astype(jnp.bfloat16)
-    for copy in copies[1:]:
+    for copy in copies[1:-2]:
         copy.wait()
     live = (lax.broadcasted_iota(jnp.int32, (1, pairs), 1) < live_ref[0]).astype(jnp.float32)
     stick = stick_ref[...].astype(jnp.float32)
     weights = (stiff_ref[...] * live) * (stick + (1.0 - stick) * slip_ref[...])
+    w_rows = RECORD + W_HIGH
+    w_sums = transform(table_ref, 0, w_rows, weights)
+    copies[-2].wait()
     forces = force_ref[...] * live
-    sums = jnp.dot(
-        table_ref[...],
-        jnp.concatenate([weights, forces], axis=0),
-        precision=lax.Precision.HIGHEST,
-        preferred_element_type=jnp.float32,
-    )
-    low, high = sums[:LANES], sums[LANES:]
+    f_rows = RECORD - F_START
+    f_sums = transform(table_ref, w_rows, w_rows + 2 * f_rows, forces)
+
+    def rows(count):
+        return jnp.zeros((count, pairs), jnp.float32)
+
+    low = w_sums[:RECORD] + jnp.concatenate([rows(F_START), f_sums[:f_rows]], axis=0)
+    high = jnp.concatenate([w_sums[RECORD:], rows(RECORD - W_HIGH)], axis=0) + jnp.concatenate(
+        [rows(F_START), f_sums[f_rows:]], axis=0
+    )
+    lane = lax.broadcasted_iota(jnp.int32, (RECORD, pairs), 0)
+    is_w, is_value = lane < W_LANES, lane < MEAN
     size = jnp.maximum(jnp.abs(low), jnp.abs(high))
-    step_w = scale_step(jnp.max(size[:W_LANES], axis=0, keepdims=True))
-    step_f = scale_step(jnp.max(size[W_LANES:MEAN], axis=0, keepdims=True))
-    lane = lax.broadcasted_iota(jnp.int32, (LANES, pairs), 0)
+    step_w = scale_step(jnp.max(jnp.where(is_w, size, 0.0), axis=0, keepdims=True))
+    step_f = scale_step(jnp.max(jnp.where(is_value & ~is_w, size, 0.0), axis=0, keepdims=True))
     factor = jnp.where(
-        lane < W_LANES, jnp.exp2(step_w * (-1.0 / STEPS)) * TOP, jnp.exp2(step_f * (-1.0 / STEPS)) * TOP
-    )
-    mean = jnp.round(sums[MEAN : MEAN + 1] * MEAN_PAIR).astype(jnp.int32)
-    low = jnp.round(low * jnp.where(lane < MEAN, factor, 0.0)).astype(jnp.int32)
+        is_w, jnp.exp2(step_w * (-1.0 / STEPS)) * TOP, jnp.exp2(step_f * (-1.0 / STEPS)) * TOP
+    )
+    factor = jnp.where(is_value, factor, 0.0)
+    mean = jnp.round(low[MEAN : MEAN + 1] * MEAN_PAIR).astype(jnp.int32)
+    low = jnp.round(low * factor).astype(jnp.int32)
     low = jnp.where(lane == MEAN, ((mean & 0xFFFF) ^ 0x8000) - 0x8000, low)
     low = jnp.where(lane == EXP_W, step_w.astype(jnp.int32), low)
     low = jnp.where(lane == EXP_F, step_f.astype(jnp.int32), low)
-    high = jnp.round(high * jnp.where(lane < MEAN, factor, 0.0)).astype(jnp.int32)
+    high = jnp.round(high * factor).astype(jnp.int32)
     high = jnp.where(lane == MEAN, mean >> 16, high)
-    both = jnp.concatenate([low, high], axis=0)
+    free = jnp.zeros((FREE, pairs), jnp.int32)
+    both = jnp.concatenate([low, free, high, free], axis=0)
     digits = jnp.concatenate([both >> 8, both & 255], axis=0).astype(jnp.float32).astype(jnp.bfloat16)
     sent = lax.dot_general(
         pick, digits, (((1,), (1,)), ((), ())), preferred_element_type=jnp.float32
@@ -191,8 +226,15 @@
     value_low = (sent[:, :LANES] * 256.0 + sent[:, 2 * LANES : 3 * LANES]).astype(jnp.int32)
     value_high = (sent[:, LANES : 2 * LANES] * 256.0 + sent[:, 3 * LANES :]).astype(jnp.int32)
     words = (value_high << 16) | (value_low & 0xFFFF)
-    word_lane = lax.broadcasted_iota(jnp.int32, (SLOTS, LANES), 1)
-    out_ref[...] = jnp.where(word_lane == NODE, node, words)
+    words = jnp.where(lax.broadcasted_iota(jnp.int32, (SLOTS, LANES), 1) == NODE, node, words)
+    last = words[ROWS * N_FIRST :]
+    own = lax.broadcasted_iota(jnp.int32, (N_FIRST, LANES), 1) < RECORD
+    for k in range(ROWS):
+        spread = pltpu.roll(last, RECORD - FREE * k, 1)
+        out_ref[pl.ds(k, N_FIRST, stride=ROWS), :] = jnp.where(
+            own, words[k * N_FIRST : (k + 1) * N_FIRST], spread
+        )
+    copies[-1].wait()
 
 
 def decode(words, mean_unit):
@@ -220,10 +262,15 @@
 
 
 def merge_kernel(words_ref, out_ref):
-    words = words_ref[...]
+    lane = lax.broadcasted_iota(jnp.int32, (N_FIRST, LANES), 1)
+    records = [words_ref[pl.ds(k, N_FIRST, stride=ROWS), :] for k in range(ROWS)]
+    last = pltpu.roll(records[0], FREE, 1)
+    for k in range(1, ROWS):
+        last = jnp.where(lane < FREE * k, last, pltpu.roll(records[k], FREE * (k + 1), 1))
+    words = jnp.concatenate(records + [last], axis=0)
     values = decode(words, MEAN_PAIR)
     rows = N_REST * NODE_DEV
-    place = lax.broadcasted_iota(jnp.int32, (SLOTS, 1), 0) % GROUP // CAP
+    place = lax.broadcasted_iota(jnp.int32, (SLOTS, 1), 0) // (CAP * N_FIRST)
     node = words[:, NODE : NODE + 1]
     node = jnp.where(node >= 0, node + place * NODE_DEV, -1)
     owner = lax.broadcasted_iota(jnp.int32, (SLOTS, rows), 1) == node
@@ -254,18 +301,14 @@
             out_ref[start : start + NODE_DEV] = words[part * NODE_DEV : (part + 1) * NODE_DEV]
 
 
-def expand_kernel(words_ref, table_ref, out_ref, held_ref, sem):
-    harm = lax.axis_index("h")
-    copy = pltpu.make_async_copy(table_ref.at[harm], held_ref, sem)
-    copy.start()
+def expand_kernel(words_ref, table_ref, out_ref):
     nodes = N_HARM * NODE_DEV
     values = decode(words_ref[:nodes], MEAN_NODE)
     for part in range(1, N_REST):
         values += decode(words_ref[part * nodes : (part + 1) * nodes], MEAN_NODE)
     terms = jnp.concatenate(split_terms(values, 2), axis=0)
-    copy.wait()
     blocks = lax.dot_general(
-        held_ref[...], terms, (((1,), (1,)), ((), ())), preferred_element_type=jnp.float32
+        table_ref[...], terms, (((1,), (1,)), ((), ())), preferred_element_type=jnp.float32
     )
     blocks = (blocks[:, :nodes] + blocks[:, nodes:]).reshape(PER, PAD, nodes)
     out_ref[...] = blocks[:, :COEFS].astype(jnp.bfloat16)
@@ -280,19 +323,23 @@
     vmem = pl.BlockSpec(memory_space=pltpu.VMEM)
     hbm = pl.BlockSpec(memory_space=pltpu.HBM)
     params = pltpu.CompilerParams(vmem_limit_bytes=32 * 1024 * 1024)
-    slots = pl.pallas_call(
+    analysis = analysis_table()
+    slots, synthesis = pl.pallas_call(
         send_kernel,
-        out_shape=jax.ShapeDtypeStruct((SLOTS, LANES), jnp.int32),
-        in_specs=[pl.BlockSpec(memory_space=pltpu.SMEM)] + [hbm] * 6,
-        out_specs=vmem,
+        out_shape=(
+            jax.ShapeDtypeStruct((ROWS * N_FIRST, LANES), jnp.int32),
+            jax.ShapeDtypeStruct((T_ROWS, 2 * LANES), jnp.bfloat16),
+        ),
+        in_specs=[pl.BlockSpec(memory_space=pltpu.SMEM)] + [hbm] * 7,
+        out_specs=(vmem, vmem),
         scratch_shapes=[
             pltpu.VMEM((SAMPLES, pairs), jnp.int32),
             pltpu.VMEM((1, pairs), jnp.float32),
             pltpu.VMEM((SAMPLES, pairs), jnp.float32),
             pltpu.VMEM((SAMPLES, pairs), jnp.float32),
             pltpu.VMEM((2, pairs), jnp.int32),
-            pltpu.VMEM((2 * LANES, 2 * SAMPLES), jnp.float32),
-            pltpu.SemaphoreType.DMA((6,)),
+            pltpu.VMEM(analysis.shape, jnp.bfloat16),
+            pltpu.SemaphoreType.DMA((7,)),
         ],
         compiler_params=params,
     )(
@@ -302,27 +349,27 @@
         in_hbm(slip_tangent),
         in_hbm(contact_force),
         in_hbm(owner_node),
-        in_hbm(jnp.asarray(analysis_table())),
-    )
-    slots = lax.all_to_all(slots.reshape(N_FIRST, 1, GROUP * LANES), FIRST, 0, 0, tiled=True)
+        in_hbm(jnp.asarray(analysis)),
+        in_hbm(jnp.asarray(synthesis_table())),
+    )
+    slots = lax.all_to_all(slots.reshape(N_FIRST, 1, ROWS * LANES), FIRST, 0, 0, tiled=True)
     sums = pl.pallas_call(
         merge_kernel,
         out_shape=jax.ShapeDtypeStruct((N_REST * N_HARM * NODE_DEV, LANES), jnp.int32),
         in_specs=[vmem],
         out_specs=vmem,
         compiler_params=params,
-    )(slots.reshape(SLOTS, LANES))
+    )(slots.reshape(ROWS * N_FIRST, LANES))
     sums = lax.all_to_all(
         sums.reshape(N_REST * N_HARM, NODE_DEV, LANES), REST + ("h",), 0, 0, tiled=True
     )
     blocks = pl.pallas_call(
         expand_kernel,
         out_shape=jax.ShapeDtypeStruct((PER, COEFS, N_HARM * NODE_DEV), jnp.bfloat16),
-        in_specs=[vmem, hbm],
+        in_specs=[vmem, vmem],
         out_specs=vmem,
-        scratch_shapes=[pltpu.VMEM((T_ROWS, 2 * LANES), jnp.bfloat16), pltpu.SemaphoreType.DMA],
         compiler_params=params,
-    )(sums.reshape(N_REST * N_HARM * NODE_DEV, LANES), in_hbm(jnp.asarray(synthesis_table())))
+    )(sums.reshape(N_REST * N_HARM * NODE_DEV, LANES), synthesis)
     return jnp.transpose(blocks, (1, 0, 2))
 
 

time: 53.7 us -> 51 us (0.950)
  Pallas kernels: 5.29 us -> 3.88 us
  blocking collectives: 47.5 us -> 46.3 us
    all_to_all x1, blocking collectives: 35.6 us -> 34 us  [on_device(): lax.all_to_all(slots.reshape(N_FIRST, 1, ROWS * LANES), FIRST, 0, 0, tile...]
    pallas_call x1, Pallas kernels: 2.18 us -> 1.23 us  [on_device(): pl.pallas_call(expand_kernel, out_shape=jax.ShapeDtypeStruct((PER, COEFS,...]
where the time goes in v5:
time: 51 us; the launch traced here: 50.8 us
  blocking collectives  46.3 us (91%)
  Pallas kernels  3.88 us (8%)
  between operations  0.67 us (1%)
    all_to_all x1, blocking collectives, on_device(): lax.all_to_all(slots.reshape(N_FIRST, 1, ROWS * LANES), FIRST, 0, 0, tile...  34 us
    all_to_all x1, blocking collectives, on_device(): lax.all_to_all(sums.reshape(N_REST * N_HARM, NODE_DEV, LANES), REST + ('h...  12.3 us
    pallas_call x1, Pallas kernels, on_device(): pl.pallas_call(send_kernel, out_shape=(jax.ShapeDtypeStruct((ROWS * N_FIR...  1.99 us
    pallas_call x1, Pallas kernels, on_device(): pl.pallas_call(expand_kernel, out_shape=jax.ShapeDtypeStruct((PER, COEFS,...  1.23 us

profile of v5, /device:TPU:1, one launch (start us, length us, event | category | flops | bytes accessed | tf_op | source)
XLA Modules:
  0.0 50.8 jit_solution(14046769139424984063)
XLA Ops:
  0.7 2.0 %shard_map.82 = (s32[320,128]{1,0:T(8,128)S(1)}, bf16[1224,256]{1,0:T(8,128)(2,1)S(1)}) custom-call(s32[1]{0:T(128)S(6)} %copy.10.live_ref, s32[256,128]{1,0:T(8,128)} %stick_hbm.1, f32[1,128]{1,0:T(1,128)} %bitcast.10, f32[256,128]{1,0:T(8,128)} %slip_hbm.1, f32[256,128]{1,0:T(8,128)} %force_hbm.1, s32[2,128]{1,0:T(2,128)} %owner_hbm.1, ...), custom_call_target="tpu_custom_call" | custom-call | tf_op jit(solution)/shard_map/pallas_call | solution.py:327
  2.7 34.0 %all_to_all.10 = s32[64,1,640]{2,1,0:T(1,128)S(1)} all-to-all(s32[64,1,640]{2,1,0:T(1,128)S(1)} %bitcast.9), channel_id=1, replica_groups=mesh['x'=4,'z'=16,'c'=2,'h'=4] {'x','z'}, dimensions={0} | all-to-all | bytes 327680 | tf_op jit(solution)/shard_map/all_to_all | solution.py:355
  36.7 0.7 %shard_map.83 = s32[256,128]{1,0:T(8,128)S(1)} custom-call(s32[320,128]{1,0:T(8,128)S(1)} %bitcast.6), custom_call_target="tpu_custom_call" | custom-call | tf_op jit(solution)/shard_map/pallas_call | solution.py:356
  37.3 12.3 %all_to_all.11 = s32[8,32,128]{2,1,0:T(8,128)S(1)} all-to-all(s32[8,32,128]{2,1,0:T(8,128)S(1)} %bitcast.7), channel_id=1, replica_groups=mesh['x'=4,'z'=16,'c'=2,'h'=4] {'c','h'}, dimensions={0} | all-to-all | bytes 262144 | tf_op jit(solution)/shard_map/all_to_all | solution.py:363
  49.6 1.2 %shard_map.84 = bf16[17,67,128]{2,1,0:T(8,128)(2,1)} custom-call(s32[256,128]{1,0:T(8,128)S(1)} %bitcast.8, bf16[1224,256]{1,0:T(8,128)(2,1)S(1)} %get-tuple-element.8.table_ref), custom_call_target="tpu_custom_call" | custom-call | tf_op jit(solution)/shard_map/pallas_call | solution.py:366

commit v6 on v5

--- a/solution.py
+++ b/solution.py
@@ -14,12 +14,10 @@
 SAMPLES = 256
 NODE_DEV = 32
 CAP = 3
-SIZES = {"x": 4, "z": 16, "c": 2, "h": 4}
-FIRST = ("x", "z")
-REST = tuple(axis for axis in ("x", "z", "c") if axis not in FIRST)
-N_FIRST = math.prod(SIZES[axis] for axis in FIRST)
-N_REST = math.prod(SIZES[axis] for axis in REST)
-N_HARM = SIZES["h"]
+N_X, N_Z, N_REST, N_HARM = 4, 16, 2, 4
+N_FIRST = N_X * N_Z
+Z_STEP = 9
+PEERS = [x * N_Z + place * Z_STEP % N_Z for place in range(N_Z) for x in range(N_X)]
 GROUP = N_REST * CAP
 SLOTS = N_FIRST * GROUP
 
@@ -100,13 +98,6 @@
                 add(row, "s", a + b, half)
                 add(row, "s", b - a, half)
     return table.reshape(N_HARM, T_ROWS, 2 * LANES).astype(jnp.bfloat16)
-
-
-def index_along(axes, part):
-    index = 0
-    for axis in axes:
-        index = index * SIZES[axis] + part[axis]
-    return index
 
 
 def scale_step(largest):
@@ -169,12 +160,8 @@
     place_second = jnp.sum(count_second, axis=0, keepdims=True)
 
     def slot_of(dest, place):
-        part = {
-            "x": dest // (SIZES["z"] * SIZES["c"]),
-            "z": dest // SIZES["c"] % SIZES["z"],
-            "c": dest % SIZES["c"],
-        }
-        return (index_along(REST, part) * CAP + place) * N_FIRST + index_along(FIRST, part)
+        x, z, core = dest // (N_Z * N_REST), dest // N_REST % N_Z, dest % N_REST
+        return (core * CAP + place) * N_FIRST + z * Z_STEP % N_Z * N_X + x
 
     slot = lax.broadcasted_iota(jnp.int32, (SLOTS, pairs), 0)
     hit_first = slot == slot_of(first, place_first)
@@ -352,7 +339,9 @@
         in_hbm(jnp.asarray(analysis)),
         in_hbm(jnp.asarray(synthesis_table())),
     )
-    slots = lax.all_to_all(slots.reshape(N_FIRST, 1, ROWS * LANES), FIRST, 0, 0, tiled=True)
+    slots = lax.all_to_all(
+        slots.reshape(N_FIRST, 1, ROWS * LANES), "xz", 0, 0, tiled=True, axis_index_groups=[PEERS]
+    )
     sums = pl.pallas_call(
         merge_kernel,
         out_shape=jax.ShapeDtypeStruct((N_REST * N_HARM * NODE_DEV, LANES), jnp.int32),
@@ -361,7 +350,7 @@
         compiler_params=params,
     )(slots.reshape(ROWS * N_FIRST, LANES))
     sums = lax.all_to_all(
-        sums.reshape(N_REST * N_HARM, NODE_DEV, LANES), REST + ("h",), 0, 0, tiled=True
+        sums.reshape(N_REST * N_HARM, NODE_DEV, LANES), ("c", "h"), 0, 0, tiled=True
     )
     blocks = pl.pallas_call(
         expand_kernel,
@@ -374,12 +363,12 @@
 
 
 def solution(mesh):
-    fine = Mesh(mesh.devices.reshape(tuple(SIZES.values())), tuple(SIZES))
-    every = ("x", "z", "c", "h")
+    fine = Mesh(mesh.devices.reshape(N_FIRST, N_REST, N_HARM), ("xz", "c", "h"))
+    every = ("xz", "c", "h")
     return jax.shard_map(
         on_device,
         mesh=fine,
         in_specs=(P(None, every), P(every), P(None, every), P(None, every), P(None, every), P(every)),
-        out_specs=P(None, "h", ("x", "z", "c")),
+        out_specs=P(None, "h", ("xz", "c")),
         check_vma=False,
     )

time: 51 us -> 53 us (1.039)
  blocking collectives: 46.3 us -> 48.3 us
    all_to_all x2, blocking collectives: 46.3 us -> 48.3 us  [the longest x1 35.6 us: on_device(): lax.all_to_all(slots.reshape(N_FIRST, 1, ROWS * LANES), 'xz', 0, 0, tiled...]
where the time goes in v6:
time: 53 us; the launch traced here: 52.8 us
  blocking collectives  48.3 us (91%)
  Pallas kernels  3.88 us (7%)
  between operations  0.67 us (1%)
    all_to_all x1, blocking collectives, on_device(): lax.all_to_all(slots.reshape(N_FIRST, 1, ROWS * LANES), 'xz', 0, 0, tiled...  35.6 us
    all_to_all x1, blocking collectives, on_device(): lax.all_to_all(sums.reshape(N_REST * N_HARM, NODE_DEV, LANES), ('c', 'h')...  12.6 us
    pallas_call x1, Pallas kernels, on_device(): pl.pallas_call(send_kernel, out_shape=(jax.ShapeDtypeStruct((ROWS * N_FIR...  1.99 us
    pallas_call x1, Pallas kernels, on_device(): pl.pallas_call(expand_kernel, out_shape=jax.ShapeDtypeStruct((PER, COEFS,...  1.23 us

profile of v6, /device:TPU:1, one launch (start us, length us, event | category | flops | bytes accessed | tf_op | source)
XLA Modules:
  0.0 52.8 jit_solution(3874755177727292735)
XLA Ops:
  0.7 2.0 %shard_map.82 = (s32[320,128]{1,0:T(8,128)S(1)}, bf16[1224,256]{1,0:T(8,128)(2,1)S(1)}) custom-call(s32[1]{0:T(128)S(6)} %copy.10.live_ref, s32[256,128]{1,0:T(8,128)} %stick_hbm.1, f32[1,128]{1,0:T(1,128)} %bitcast.10, f32[256,128]{1,0:T(8,128)} %slip_hbm.1, f32[256,128]{1,0:T(8,128)} %force_hbm.1, s32[2,128]{1,0:T(2,128)} %owner_hbm.1, ...), custom_call_target="tpu_custom_call" | custom-call | tf_op jit(solution)/shard_map/pallas_call | solution.py:314
  2.7 35.6 %all_to_all.10 = s32[64,1,640]{2,1,0:T(1,128)S(1)} all-to-all(s32[64,1,640]{2,1,0:T(1,128)S(1)} %bitcast.9), channel_id=1, replica_groups={{0,128,256,384,72,200,328,456,16,144,272,400,88,216,344,472,32,160,288,..., dimensions={0} | all-to-all | bytes 327680 | tf_op jit(solution)/shard_map/all_to_all | solution.py:342
  38.3 0.7 %shard_map.83 = s32[256,128]{1,0:T(8,128)S(1)} custom-call(s32[320,128]{1,0:T(8,128)S(1)} %bitcast.6), custom_call_target="tpu_custom_call" | custom-call | tf_op jit(solution)/shard_map/pallas_call | solution.py:345
  39.0 12.6 %all_to_all.11 = s32[8,32,128]{2,1,0:T(8,128)S(1)} all-to-all(s32[8,32,128]{2,1,0:T(8,128)S(1)} %bitcast.7), channel_id=1, replica_groups=mesh['xz'=64,'c'=2,'h'=4] {'c','h'}, dimensions={0} | all-to-all | bytes 262144 | tf_op jit(solution)/shard_map/all_to_all | solution.py:352
  51.6 1.2 %shard_map.84 = bf16[17,67,128]{2,1,0:T(8,128)(2,1)} custom-call(s32[256,128]{1,0:T(8,128)S(1)} %bitcast.8, bf16[1224,256]{1,0:T(8,128)(2,1)S(1)} %get-tuple-element.8.table_ref), custom_call_target="tpu_custom_call" | custom-call | tf_op jit(solution)/shard_map/pallas_call | solution.py:355

commit v7 on v6

--- a/solution.py
+++ b/solution.py
@@ -16,20 +16,23 @@
 CAP = 3
 N_X, N_Z, N_REST, N_HARM = 4, 16, 2, 4
 N_FIRST = N_X * N_Z
-Z_STEP = 9
-PEERS = [x * N_Z + place * Z_STEP % N_Z for place in range(N_Z) for x in range(N_X)]
+X_FIRST, Z_FIRST = 2, 9
+PEERS = [
+    (X_FIRST + x) % N_X * N_Z + (Z_FIRST + z) % N_Z for x in range(N_X) for z in range(N_Z)
+]
 GROUP = N_REST * CAP
 SLOTS = N_FIRST * GROUP
 
 LANES = 128
 W_LANES = 66
-F_LOW = 34
 MEAN, EXP_W, EXP_F, NODE = 100, 101, 102, 103
 RECORD = 104
 F_START = 64
 ROWS = GROUP - 1
 FREE = LANES - RECORD
-W_HIGH = 72
+HALF = SAMPLES // 2
+W_LOW, F_ROWS, W_HIGH = 80, 48, 112
+TABLE = W_LOW + F_ROWS + W_HIGH + F_ROWS
 STEPS = 16.0
 TOP = 32766.0
 MEAN_PAIR = 2.0**21
@@ -39,24 +42,39 @@
 T_ROWS = PER * PAD
 
 
+def weight_lane(sine, k):
+    return (k % 2 == 0) * LANES + (k - 1) // 2 + sine * HARMONICS
+
+
+def force_lane(sine, k):
+    if k % 2:
+        return W_LANES + (k - 1) // 2 + sine * (HARMONICS // 2 + 1)
+    return LANES + W_LANES + k // 2 + sine * (HARMONICS // 2)
+
+
 def analysis_table():
     k = np.arange(HARMONICS * 2 + 1)[:, None]
-    angle = (k * np.arange(SAMPLES)[None, :] % SAMPLES) * (2.0 * np.pi / SAMPLES)
-    cosine, sine = np.cos(angle), np.sin(angle)
-    basis = np.zeros((COEFS, SAMPLES))
-    basis[0] = 1.0
-    basis[1::2] = cosine[1 : HARMONICS + 1]
-    basis[2::2] = sine[1 : HARMONICS + 1]
-    w_low = np.zeros((RECORD, SAMPLES))
-    w_low[:W_LANES] = cosine[1:]
-    w_low[MEAN] = 1.0
-    w_high = np.zeros((W_HIGH, SAMPLES))
-    w_high[:W_LANES] = sine[1:]
-    f_low = np.zeros((RECORD - F_START, SAMPLES))
-    f_low[W_LANES - F_START : MEAN - F_START] = basis[:F_LOW]
-    f_high = np.zeros_like(f_low)
-    f_high[W_LANES - F_START : W_LANES - F_START + COEFS - F_LOW] = basis[F_LOW:]
-    table = np.concatenate([w_low, w_high, f_low, f_high], axis=0)
+    angle = (k * np.arange(HALF)[None, :] % SAMPLES) * (2.0 * np.pi / SAMPLES)
+    basis = np.cos(angle), np.sin(angle)
+    weights = np.zeros((2 * LANES, HALF))
+    forces = np.zeros((2 * LANES, HALF))
+    weights[LANES + MEAN] = 1.0
+    for n in range(1, 2 * HARMONICS + 1):
+        for sine in range(2):
+            weights[weight_lane(sine, n)] = basis[sine][n]
+    forces[force_lane(0, 0)] = 1.0
+    for n in range(1, HARMONICS + 1):
+        for sine in range(2):
+            forces[force_lane(sine, n)] = basis[sine][n]
+    table = np.concatenate(
+        [
+            weights[:W_LOW],
+            forces[F_START : F_START + F_ROWS],
+            weights[LANES : LANES + W_HIGH],
+            forces[LANES + F_START : LANES + F_START + F_ROWS],
+        ],
+        axis=0,
+    )
     first = table.astype(jnp.bfloat16)
     second = (table - first.astype(np.float64)).astype(jnp.bfloat16)
     return np.concatenate([first, second], axis=0)
@@ -66,22 +84,17 @@
     table = np.zeros((N_HARM, PER, PAD, 2 * LANES), np.float32)
 
     def add(row, kind, k, value):
-        if kind == "s":
-            if k == 0:
-                return
-            row[LANES + abs(k) - 1] += value if k > 0 else -value
-        elif k == 0:
-            row[MEAN] += value
+        if k == 0:
+            row[MEAN] += value * (kind == "c")
         else:
-            row[abs(k) - 1] += value
+            row[weight_lane(int(kind == "s"), abs(k))] += value if k > 0 or kind == "c" else -value
 
     for i in range(COEFS):
         a, i_sine = (i + 1) // 2, i > 0 and i % 2 == 0
         for j in range(COEFS + 1):
             row = table[j // PER, j % PER, i]
             if j == COEFS:
-                lane = W_LANES + i if i < F_LOW else LANES + W_LANES + i - F_LOW
-                row[lane] = 1.0 / math.sqrt(SAMPLES)
+                row[force_lane(int(i_sine), a)] = 1.0 / math.sqrt(SAMPLES)
                 continue
             b, j_sine = (j + 1) // 2, j > 0 and j % 2 == 0
             half = 1.0 / SAMPLES
@@ -104,16 +117,15 @@
     return jnp.ceil(jnp.log2(jnp.maximum(largest, 1e-30)) * STEPS + 0.01)
 
 
-def transform(table_ref, start, stop, samples):
-    total = table_ref.shape[0] // 2
+def transform(table_ref, start, rows, samples):
     first, second = split_terms(samples, 2)
     large = jnp.dot(
-        table_ref[start:stop],
+        table_ref[start : start + rows],
         jnp.concatenate([first, second], axis=1),
         preferred_element_type=jnp.float32,
     )
     small = jnp.dot(
-        table_ref[total + start : total + stop], first, preferred_element_type=jnp.float32
+        table_ref[TABLE + start : TABLE + start + rows], first, preferred_element_type=jnp.float32
     )
     pairs = samples.shape[1]
     return large[:, :pairs] + (large[:, pairs:] + small)
@@ -161,7 +173,8 @@
 
     def slot_of(dest, place):
         x, z, core = dest // (N_Z * N_REST), dest // N_REST % N_Z, dest % N_REST
-        return (core * CAP + place) * N_FIRST + z * Z_STEP % N_Z * N_X + x
+        rank = (x + (N_X - X_FIRST)) % N_X * N_Z + (z + (N_Z - Z_FIRST)) % N_Z
+        return (core * CAP + place) * N_FIRST + rank
 
     slot = lax.broadcasted_iota(jnp.int32, (SLOTS, pairs), 0)
     hit_first = slot == slot_of(first, place_first)
@@ -174,20 +187,23 @@
     live = (lax.broadcasted_iota(jnp.int32, (1, pairs), 1) < live_ref[0]).astype(jnp.float32)
     stick = stick_ref[...].astype(jnp.float32)
     weights = (stiff_ref[...] * live) * (stick + (1.0 - stick) * slip_ref[...])
-    w_rows = RECORD + W_HIGH
-    w_sums = transform(table_ref, 0, w_rows, weights)
+    low = transform(table_ref, 0, W_LOW, weights[:HALF] - weights[HALF:])
+    high = transform(table_ref, W_LOW + F_ROWS, W_HIGH, weights[:HALF] + weights[HALF:])
     copies[-2].wait()
     forces = force_ref[...] * live
-    f_rows = RECORD - F_START
-    f_sums = transform(table_ref, w_rows, w_rows + 2 * f_rows, forces)
+    f_low = transform(table_ref, W_LOW, F_ROWS, forces[:HALF] - forces[HALF:])
+    f_high = transform(
+        table_ref, W_LOW + F_ROWS + W_HIGH, F_ROWS, forces[:HALF] + forces[HALF:]
+    )
 
     def rows(count):
         return jnp.zeros((count, pairs), jnp.float32)
 
-    low = w_sums[:RECORD] + jnp.concatenate([rows(F_START), f_sums[:f_rows]], axis=0)
-    high = jnp.concatenate([w_sums[RECORD:], rows(RECORD - W_HIGH)], axis=0) + jnp.concatenate(
-        [rows(F_START), f_sums[f_rows:]], axis=0
-    )
+    f_end = RECORD - F_START
+    low = jnp.concatenate([low, rows(RECORD - W_LOW)], axis=0) + jnp.concatenate(
+        [rows(F_START), f_low[:f_end]], axis=0
+    )
+    high = high[:RECORD] + jnp.concatenate([rows(F_START), f_high[:f_end]], axis=0)
     lane = lax.broadcasted_iota(jnp.int32, (RECORD, pairs), 0)
     is_w, is_value = lane < W_LANES, lane < MEAN
     size = jnp.maximum(jnp.abs(low), jnp.abs(high))
@@ -197,7 +213,7 @@
         is_w, jnp.exp2(step_w * (-1.0 / STEPS)) * TOP, jnp.exp2(step_f * (-1.0 / STEPS)) * TOP
     )
     factor = jnp.where(is_value, factor, 0.0)
-    mean = jnp.round(low[MEAN : MEAN + 1] * MEAN_PAIR).astype(jnp.int32)
+    mean = jnp.round(high[MEAN : MEAN + 1] * MEAN_PAIR).astype(jnp.int32)
     low = jnp.round(low * factor).astype(jnp.int32)
     low = jnp.where(lane == MEAN, ((mean & 0xFFFF) ^ 0x8000) - 0x8000, low)
     low = jnp.where(lane == EXP_W, step_w.astype(jnp.int32), low)
@@ -262,12 +278,12 @@
     node = jnp.where(node >= 0, node + place * NODE_DEV, -1)
     owner = lax.broadcasted_iota(jnp.int32, (SLOTS, rows), 1) == node
     owner = jnp.where(owner, 1.0, 0.0).astype(jnp.bfloat16)
-    terms = jnp.concatenate(split_terms(values, 3), axis=1)
+    terms = jnp.concatenate(split_terms(values, 2), axis=1)
     total = lax.dot_general(
         owner, terms, (((0,), (0,)), ((), ())), preferred_element_type=jnp.float32
     )
-    low = total[:, :LANES] + (total[:, 2 * LANES : 3 * LANES] + total[:, 4 * LANES : 5 * LANES])
-    high = total[:, LANES : 2 * LANES] + (total[:, 3 * LANES : 4 * LANES] + total[:, 5 * LANES :])
+    low = total[:, :LANES] + total[:, 2 * LANES : 3 * LANES]
+    high = total[:, LANES : 2 * LANES] + total[:, 3 * LANES :]
     size = jnp.maximum(jnp.abs(low), jnp.abs(high))
     lane = lax.broadcasted_iota(jnp.int32, size.shape, 1)
     step_w = scale_step(jnp.max(jnp.where(lane < W_LANES, size, 0.0), axis=1, keepdims=True))

time: 53 us -> 45.2 us (0.85)
  blocking collectives: 48.3 us -> 40.6 us
    all_to_all x1, blocking collectives: 35.6 us -> 30.3 us  [on_device(): lax.all_to_all(slots.reshape(N_FIRST, 1, ROWS * LANES), 'xz', 0, 0, tiled...]
    all_to_all x1, blocking collectives: 12.6 us -> 10.3 us  [on_device(): lax.all_to_all(sums.reshape(N_REST * N_HARM, NODE_DEV, LANES), ('c', 'h')...]
where the time goes in v7:
time: 45.2 us; the launch traced here: 45 us
  blocking collectives  40.6 us (90%)
  Pallas kernels  3.77 us (8%)
  between operations  0.67 us (1%)
    all_to_all x1, blocking collectives, on_device(): lax.all_to_all(slots.reshape(N_FIRST, 1, ROWS * LANES), 'xz', 0, 0, tiled...  30.3 us
    all_to_all x1, blocking collectives, on_device(): lax.all_to_all(sums.reshape(N_REST * N_HARM, NODE_DEV, LANES), ('c', 'h')...  10.3 us
    pallas_call x1, Pallas kernels, on_device(): pl.pallas_call(send_kernel, out_shape=(jax.ShapeDtypeStruct((ROWS * N_FIR...  1.95 us
    pallas_call x1, Pallas kernels, on_device(): pl.pallas_call(expand_kernel, out_shape=jax.ShapeDtypeStruct((PER, COEFS,...  1.24 us

profile of v7, /device:TPU:1, one launch (start us, length us, event | category | flops | bytes accessed | tf_op | source)
XLA Modules:
  0.0 45.0 jit_solution(9403259145480478114)
XLA Ops:
  0.7 2.0 %shard_map.82 = (s32[320,128]{1,0:T(8,128)S(1)}, bf16[1224,256]{1,0:T(8,128)(2,1)S(1)}) custom-call(s32[1]{0:T(128)S(6)} %copy.10.live_ref, s32[256,128]{1,0:T(8,128)} %stick_hbm.1, f32[1,128]{1,0:T(1,128)} %bitcast.10, f32[256,128]{1,0:T(8,128)} %slip_hbm.1, f32[256,128]{1,0:T(8,128)} %force_hbm.1, s32[2,128]{1,0:T(2,128)} %owner_hbm.1, ...), custom_call_target="tpu_custom_call" | custom-call | tf_op jit(solution)/shard_map/pallas_call | solution.py:330
  2.6 30.3 %all_to_all.10 = s32[64,1,640]{2,1,0:T(1,128)S(1)} all-to-all(s32[64,1,640]{2,1,0:T(1,128)S(1)} %bitcast.9), channel_id=1, replica_groups={{328,336,344,352,360,368,376,256,264,272,280,288,296,304,312,320,456,46..., dimensions={0} | all-to-all | bytes 327680 | tf_op jit(solution)/shard_map/all_to_all | solution.py:358
  32.9 0.6 %shard_map.83 = s32[256,128]{1,0:T(8,128)S(1)} custom-call(s32[320,128]{1,0:T(8,128)S(1)} %bitcast.6), custom_call_target="tpu_custom_call" | custom-call | tf_op jit(solution)/shard_map/pallas_call | solution.py:361
  33.5 10.3 %all_to_all.11 = s32[8,32,128]{2,1,0:T(8,128)S(1)} all-to-all(s32[8,32,128]{2,1,0:T(8,128)S(1)} %bitcast.7), channel_id=1, replica_groups=mesh['xz'=64,'c'=2,'h'=4] {'c','h'}, dimensions={0} | all-to-all | bytes 262144 | tf_op jit(solution)/shard_map/all_to_all | solution.py:368
  43.8 1.2 %shard_map.84 = bf16[17,67,128]{2,1,0:T(8,128)(2,1)} custom-call(s32[256,128]{1,0:T(8,128)S(1)} %bitcast.8, bf16[1224,256]{1,0:T(8,128)(2,1)S(1)} %get-tuple-element.8.table_ref), custom_call_target="tpu_custom_call" | custom-call | tf_op jit(solution)/shard_map/pallas_call | solution.py:371

commit v8 on v7

--- a/solution.py
+++ b/solution.py
@@ -20,6 +20,9 @@
 PEERS = [
     (X_FIRST + x) % N_X * N_Z + (Z_FIRST + z) % N_Z for x in range(N_X) for z in range(N_Z)
 ]
+H_FIRST = 2
+CORES = (1, 0)
+MEMBERS = [core * N_HARM + (H_FIRST + h) % N_HARM for core in CORES for h in range(N_HARM)]
 GROUP = N_REST * CAP
 SLOTS = N_FIRST * GROUP
 
@@ -298,10 +301,9 @@
     words = jnp.where(lane == MEAN, jnp.round(low * MEAN_NODE).astype(jnp.int32), words)
     words = jnp.where(lane == EXP_W, step_w.astype(jnp.int32), words)
     words = jnp.where(lane == EXP_F, step_f.astype(jnp.int32), words)
-    for part in range(N_REST):
-        for harm in range(N_HARM):
-            start = (part * N_HARM + harm) * NODE_DEV
-            out_ref[start : start + NODE_DEV] = words[part * NODE_DEV : (part + 1) * NODE_DEV]
+    for rank, member in enumerate(MEMBERS):
+        start = member // N_HARM * NODE_DEV
+        out_ref[rank * NODE_DEV : (rank + 1) * NODE_DEV] = words[start : start + NODE_DEV]
 
 
 def expand_kernel(words_ref, table_ref, out_ref):
@@ -309,6 +311,8 @@
     values = decode(words_ref[:nodes], MEAN_NODE)
     for part in range(1, N_REST):
         values += decode(words_ref[part * nodes : (part + 1) * nodes], MEAN_NODE)
+    wrap = (N_HARM - H_FIRST) * NODE_DEV
+    values = jnp.concatenate([values[wrap:], values[:wrap]], axis=0)
     terms = jnp.concatenate(split_terms(values, 2), axis=0)
     blocks = lax.dot_general(
         table_ref[...], terms, (((1,), (1,)), ((), ())), preferred_element_type=jnp.float32
@@ -366,7 +370,12 @@
         compiler_params=params,
     )(slots.reshape(ROWS * N_FIRST, LANES))
     sums = lax.all_to_all(
-        sums.reshape(N_REST * N_HARM, NODE_DEV, LANES), ("c", "h"), 0, 0, tiled=True
+        sums.reshape(N_REST * N_HARM, NODE_DEV, LANES),
+        ("c", "h"),
+        0,
+        0,
+        tiled=True,
+        axis_index_groups=[MEMBERS],
     )
     blocks = pl.pallas_call(
         expand_kernel,

time: 45.2 us -> 43.2 us (0.956)
  blocking collectives: 40.6 us -> 38.5 us
    all_to_all x1, blocking collectives: 10.3 us -> 8.26 us  [on_device(): lax.all_to_all(sums.reshape(N_REST * N_HARM, NODE_DEV, LANES), ('c', 'h')...]
where the time goes in v8:
time: 43.2 us; the launch traced here: 43 us
  blocking collectives  38.5 us (89%)
  Pallas kernels  3.77 us (9%)
  between operations  0.67 us (2%)
    all_to_all x1, blocking collectives, on_device(): lax.all_to_all(slots.reshape(N_FIRST, 1, ROWS * LANES), 'xz', 0, 0, tiled...  30.3 us
    all_to_all x1, blocking collectives, on_device(): lax.all_to_all(sums.reshape(N_REST * N_HARM, NODE_DEV, LANES), ('c', 'h')...  8.26 us
    pallas_call x1, Pallas kernels, on_device(): pl.pallas_call(send_kernel, out_shape=(jax.ShapeDtypeStruct((ROWS * N_FIR...  1.95 us
    pallas_call x1, Pallas kernels, on_device(): pl.pallas_call(expand_kernel, out_shape=jax.ShapeDtypeStruct((PER, COEFS,...  1.24 us

profile of v8, /device:TPU:1, one launch (start us, length us, event | category | flops | bytes accessed | tf_op | source)
XLA Modules:
  0.0 43.0 jit_solution(10254771507095069474)
XLA Ops:
  0.7 2.0 %shard_map.82 = (s32[320,128]{1,0:T(8,128)S(1)}, bf16[1224,256]{1,0:T(8,128)(2,1)S(1)}) custom-call(s32[1]{0:T(128)S(6)} %copy.10.live_ref, s32[256,128]{1,0:T(8,128)} %stick_hbm.1, f32[1,128]{1,0:T(1,128)} %bitcast.10, f32[256,128]{1,0:T(8,128)} %slip_hbm.1, f32[256,128]{1,0:T(8,128)} %force_hbm.1, s32[2,128]{1,0:T(2,128)} %owner_hbm.1, ...), custom_call_target="tpu_custom_call" | custom-call | tf_op jit(solution)/shard_map/pallas_call | solution.py:334
  2.6 30.3 %all_to_all.10 = s32[64,1,640]{2,1,0:T(1,128)S(1)} all-to-all(s32[64,1,640]{2,1,0:T(1,128)S(1)} %bitcast.9), channel_id=1, replica_groups={{328,336,344,352,360,368,376,256,264,272,280,288,296,304,312,320,456,46..., dimensions={0} | all-to-all | bytes 327680 | tf_op jit(solution)/shard_map/all_to_all | solution.py:362
  32.9 0.6 %shard_map.83 = s32[256,128]{1,0:T(8,128)S(1)} custom-call(s32[320,128]{1,0:T(8,128)S(1)} %bitcast.6), custom_call_target="tpu_custom_call" | custom-call | tf_op jit(solution)/shard_map/pallas_call | solution.py:365
  33.5 8.3 %all_to_all.11 = s32[8,32,128]{2,1,0:T(8,128)S(1)} all-to-all(s32[8,32,128]{2,1,0:T(8,128)S(1)} %bitcast.7), channel_id=1, replica_groups={{6,7,4,5,2,3,0,1},{14,15,12,13,10,11,8,9},{22,23,20,21,18,19,16,17},{30..., dimensions={0} | all-to-all | bytes 262144 | tf_op jit(solution)/shard_map/all_to_all | solution.py:372
  41.8 1.2 %shard_map.84 = bf16[17,67,128]{2,1,0:T(8,128)(2,1)} custom-call(s32[256,128]{1,0:T(8,128)S(1)} %bitcast.8, bf16[1224,256]{1,0:T(8,128)(2,1)S(1)} %get-tuple-element.8.table_ref), custom_call_target="tpu_custom_call" | custom-call | tf_op jit(solution)/shard_map/pallas_call | solution.py:380

commit v9 on v8

--- a/solution.py
+++ b/solution.py
@@ -35,7 +35,6 @@
 FREE = LANES - RECORD
 HALF = SAMPLES // 2
 W_LOW, F_ROWS, W_HIGH = 80, 48, 112
-TABLE = W_LOW + F_ROWS + W_HIGH + F_ROWS
 STEPS = 16.0
 TOP = 32766.0
 MEAN_PAIR = 2.0**21
@@ -80,7 +79,7 @@
     )
     first = table.astype(jnp.bfloat16)
     second = (table - first.astype(np.float64)).astype(jnp.bfloat16)
-    return np.concatenate([first, second], axis=0)
+    return np.concatenate([first, second], axis=1)
 
 
 def synthesis_table():
@@ -122,16 +121,15 @@
 
 def transform(table_ref, start, rows, samples):
     first, second = split_terms(samples, 2)
-    large = jnp.dot(
+    upper = jnp.concatenate([first, second], axis=1)
+    lower = jnp.concatenate([first, jnp.zeros_like(first)], axis=1)
+    sums = jnp.dot(
         table_ref[start : start + rows],
-        jnp.concatenate([first, second], axis=1),
+        jnp.concatenate([upper, lower], axis=0),
         preferred_element_type=jnp.float32,
     )
-    small = jnp.dot(
-        table_ref[TABLE + start : TABLE + start + rows], first, preferred_element_type=jnp.float32
-    )
     pairs = samples.shape[1]
-    return large[:, :pairs] + (large[:, pairs:] + small)
+    return sums[:, :pairs] + sums[:, pairs:]
 
 
 def send_kernel(
@@ -184,7 +182,9 @@
     hit_second = slot == slot_of(second, place_second)
     node = jnp.where(hit_first, local[0:1] + 1, 0) + jnp.where(hit_second, local[1:2] + 1, 0)
     node = jnp.sum(node, axis=1, keepdims=True) - 1
-    pick = jnp.where(hit_first | hit_second, 1.0, 0.0).astype(jnp.bfloat16)
+    hit = hit_first | hit_second
+    pick = jnp.concatenate([jnp.where(hit, 256.0, 0.0), jnp.where(hit, 1.0, 0.0)], axis=1)
+    pick = pick.astype(jnp.bfloat16)
     for copy in copies[1:-2]:
         copy.wait()
     live = (lax.broadcasted_iota(jnp.int32, (1, pairs), 1) < live_ref[0]).astype(jnp.float32)
@@ -225,13 +225,12 @@
     high = jnp.where(lane == MEAN, mean >> 16, high)
     free = jnp.zeros((FREE, pairs), jnp.int32)
     both = jnp.concatenate([low, free, high, free], axis=0)
-    digits = jnp.concatenate([both >> 8, both & 255], axis=0).astype(jnp.float32).astype(jnp.bfloat16)
+    digits = jnp.concatenate([both >> 8, both & 255], axis=1).astype(jnp.float32).astype(jnp.bfloat16)
     sent = lax.dot_general(
         pick, digits, (((1,), (1,)), ((), ())), preferred_element_type=jnp.float32
     )
-    value_low = (sent[:, :LANES] * 256.0 + sent[:, 2 * LANES : 3 * LANES]).astype(jnp.int32)
-    value_high = (sent[:, LANES : 2 * LANES] * 256.0 + sent[:, 3 * LANES :]).astype(jnp.int32)
-    words = (value_high << 16) | (value_low & 0xFFFF)
+    sent = sent.astype(jnp.int32)
+    words = (sent[:, LANES:] << 16) | (sent[:, :LANES] & 0xFFFF)
     words = jnp.where(lax.broadcasted_iota(jnp.int32, (SLOTS, LANES), 1) == NODE, node, words)
     last = words[ROWS * N_FIRST :]
     own = lax.broadcasted_iota(jnp.int32, (N_FIRST, LANES), 1) < RECORD

time: 43.2 us -> 43.1 us (level)
  no operation moved by 1% of the time
where the time goes in v9:
time: 43.1 us; the launch traced here: 42.9 us
  blocking collectives  38.6 us (90%)
  Pallas kernels  3.69 us (9%)
  between operations  0.67 us (2%)
    all_to_all x1, blocking collectives, on_device(): lax.all_to_all(slots.reshape(N_FIRST, 1, ROWS * LANES), 'xz', 0, 0, tiled...  30.3 us
    all_to_all x1, blocking collectives, on_device(): lax.all_to_all(sums.reshape(N_REST * N_HARM, NODE_DEV, LANES), ('c', 'h')...  8.26 us
    pallas_call x1, Pallas kernels, on_device(): pl.pallas_call(send_kernel, out_shape=(jax.ShapeDtypeStruct((ROWS * N_FIR...  1.88 us
    pallas_call x1, Pallas kernels, on_device(): pl.pallas_call(expand_kernel, out_shape=jax.ShapeDtypeStruct((PER, COEFS,...  1.23 us

profile of v9, /device:TPU:1, one launch (start us, length us, event | category | flops | bytes accessed | tf_op | source)
XLA Modules:
  0.0 42.9 jit_solution(12757391978924575574)
XLA Ops:
  0.7 1.9 %shard_map.82 = (s32[320,128]{1,0:T(8,128)S(1)}, bf16[1224,256]{1,0:T(8,128)(2,1)S(1)}) custom-call(s32[1]{0:T(128)S(6)} %copy.10.live_ref, s32[256,128]{1,0:T(8,128)} %stick_hbm.1, f32[1,128]{1,0:T(1,128)} %bitcast.10, f32[256,128]{1,0:T(8,128)} %slip_hbm.1, f32[256,128]{1,0:T(8,128)} %force_hbm.1, s32[2,128]{1,0:T(2,128)} %owner_hbm.1, ...), custom_call_target="tpu_custom_call" | custom-call | tf_op jit(solution)/shard_map/pallas_call | solution.py:333
  2.5 30.3 %all_to_all.10 = s32[64,1,640]{2,1,0:T(1,128)S(1)} all-to-all(s32[64,1,640]{2,1,0:T(1,128)S(1)} %bitcast.9), channel_id=1, replica_groups={{328,336,344,352,360,368,376,256,264,272,280,288,296,304,312,320,456,46..., dimensions={0} | all-to-all | bytes 327680 | tf_op jit(solution)/shard_map/all_to_all | solution.py:361
  32.8 0.6 %shard_map.83 = s32[256,128]{1,0:T(8,128)S(1)} custom-call(s32[320,128]{1,0:T(8,128)S(1)} %bitcast.6), custom_call_target="tpu_custom_call" | custom-call | tf_op jit(solution)/shard_map/pallas_call | solution.py:364
  33.4 8.3 %all_to_all.11 = s32[8,32,128]{2,1,0:T(8,128)S(1)} all-to-all(s32[8,32,128]{2,1,0:T(8,128)S(1)} %bitcast.7), channel_id=1, replica_groups={{6,7,4,5,2,3,0,1},{14,15,12,13,10,11,8,9},{22,23,20,21,18,19,16,17},{30..., dimensions={0} | all-to-all | bytes 262144 | tf_op jit(solution)/shard_map/all_to_all | solution.py:371
  41.7 1.2 %shard_map.84 = bf16[17,67,128]{2,1,0:T(8,128)(2,1)} custom-call(s32[256,128]{1,0:T(8,128)S(1)} %bitcast.8, bf16[1224,256]{1,0:T(8,128)(2,1)S(1)} %get-tuple-element.8.table_ref), custom_call_target="tpu_custom_call" | custom-call | tf_op jit(solution)/shard_map/pallas_call | solution.py:379

commit v10 on v9

--- a/solution.py
+++ b/solution.py
@@ -16,10 +16,18 @@
 CAP = 3
 N_X, N_Z, N_REST, N_HARM = 4, 16, 2, 4
 N_FIRST = N_X * N_Z
-X_FIRST, Z_FIRST = 2, 9
-PEERS = [
-    (X_FIRST + x) % N_X * N_Z + (Z_FIRST + z) % N_Z for x in range(N_X) for z in range(N_Z)
-]
+X_FIRST = 2
+Z_FIRST = (8, 9)
+
+
+def peers(core):
+    return [
+        ((X_FIRST + x) % N_X * N_Z + (Z_FIRST[core] + z) % N_Z) * N_REST + core
+        for x in range(N_X)
+        for z in range(N_Z)
+    ]
+
+
 H_FIRST = 2
 CORES = (1, 0)
 MEMBERS = [core * N_HARM + (H_FIRST + h) % N_HARM for core in CORES for h in range(N_HARM)]
@@ -174,7 +182,8 @@
 
     def slot_of(dest, place):
         x, z, core = dest // (N_Z * N_REST), dest // N_REST % N_Z, dest % N_REST
-        rank = (x + (N_X - X_FIRST)) % N_X * N_Z + (z + (N_Z - Z_FIRST)) % N_Z
+        shift = jnp.where(lax.axis_index("c") == 0, N_Z - Z_FIRST[0], N_Z - Z_FIRST[1])
+        rank = (x + (N_X - X_FIRST)) % N_X * N_Z + (z + shift) % N_Z
         return (core * CAP + place) * N_FIRST + rank
 
     slot = lax.broadcasted_iota(jnp.int32, (SLOTS, pairs), 0)
@@ -359,7 +368,12 @@
         in_hbm(jnp.asarray(synthesis_table())),
     )
     slots = lax.all_to_all(
-        slots.reshape(N_FIRST, 1, ROWS * LANES), "xz", 0, 0, tiled=True, axis_index_groups=[PEERS]
+        slots.reshape(N_FIRST, 1, ROWS * LANES),
+        ("xz", "c"),
+        0,
+        0,
+        tiled=True,
+        axis_index_groups=[peers(core) for core in range(N_REST)],
     )
     sums = pl.pallas_call(
         merge_kernel,

time: 43.1 us -> 42.9 us (level)
  no operation moved by 1% of the time
where the time goes in v10:
time: 42.9 us; the launch traced here: 42.7 us
  blocking collectives  38.4 us (90%)
  Pallas kernels  3.7 us (9%)
  between operations  0.67 us (2%)
    all_to_all x1, blocking collectives, on_device(): lax.all_to_all(slots.reshape(N_FIRST, 1, ROWS * LANES), ('xz', 'c'), 0, 0...  30.2 us
    all_to_all x1, blocking collectives, on_device(): lax.all_to_all(sums.reshape(N_REST * N_HARM, NODE_DEV, LANES), ('c', 'h')...  8.16 us
    pallas_call x1, Pallas kernels, on_device(): pl.pallas_call(send_kernel, out_shape=(jax.ShapeDtypeStruct((ROWS * N_FIR...  1.88 us
    pallas_call x1, Pallas kernels, on_device(): pl.pallas_call(expand_kernel, out_shape=jax.ShapeDtypeStruct((PER, COEFS,...  1.23 us

profile of v10, /device:TPU:1, one launch (start us, length us, event | category | flops | bytes accessed | tf_op | source)
XLA Modules:
  0.0 42.7 jit_solution(7636056978361990817)
XLA Ops:
  0.7 1.9 %shard_map.82 = (s32[320,128]{1,0:T(8,128)S(1)}, bf16[1224,256]{1,0:T(8,128)(2,1)S(1)}) custom-call(s32[1]{0:T(128)S(6)} %copy.10.live_ref, s32[256,128]{1,0:T(8,128)} %stick_hbm.1, f32[1,128]{1,0:T(1,128)} %bitcast.10, f32[256,128]{1,0:T(8,128)} %slip_hbm.1, f32[256,128]{1,0:T(8,128)} %force_hbm.1, s32[2,128]{1,0:T(2,128)} %owner_hbm.1, ...), custom_call_target="tpu_custom_call" | custom-call | tf_op jit(solution)/shard_map/pallas_call | solution.py:342
  2.5 30.2 %all_to_all.10 = s32[64,1,640]{2,1,0:T(1,128)S(1)} all-to-all(s32[64,1,640]{2,1,0:T(1,128)S(1)} %bitcast.9), channel_id=1, replica_groups={{320,328,336,344,352,360,368,376,256,264,272,280,288,296,304,312,448,45..., dimensions={0} | all-to-all | bytes 327680 | tf_op jit(solution)/shard_map/all_to_all | solution.py:370
  32.7 0.6 %shard_map.83 = s32[256,128]{1,0:T(8,128)S(1)} custom-call(s32[320,128]{1,0:T(8,128)S(1)} %bitcast.6), custom_call_target="tpu_custom_call" | custom-call | tf_op jit(solution)/shard_map/pallas_call | solution.py:378
  33.3 8.2 %all_to_all.11 = s32[8,32,128]{2,1,0:T(8,128)S(1)} all-to-all(s32[8,32,128]{2,1,0:T(8,128)S(1)} %bitcast.7), channel_id=1, replica_groups={{6,7,4,5,2,3,0,1},{14,15,12,13,10,11,8,9},{22,23,20,21,18,19,16,17},{30..., dimensions={0} | all-to-all | bytes 262144 | tf_op jit(solution)/shard_map/all_to_all | solution.py:385
  41.5 1.2 %shard_map.84 = bf16[17,67,128]{2,1,0:T(8,128)(2,1)} custom-call(s32[256,128]{1,0:T(8,128)S(1)} %bitcast.8, bf16[1224,256]{1,0:T(8,128)(2,1)S(1)} %get-tuple-element.8.table_ref), custom_call_target="tpu_custom_call" | custom-call | tf_op jit(solution)/shard_map/pallas_call | solution.py:393

commit v11 on v10

--- a/solution.py
+++ b/solution.py
@@ -196,7 +196,7 @@
     pick = pick.astype(jnp.bfloat16)
     for copy in copies[1:-2]:
         copy.wait()
-    live = (lax.broadcasted_iota(jnp.int32, (1, pairs), 1) < live_ref[0]).astype(jnp.float32)
+    live = (lax.broadcasted_iota(jnp.int32, (1, pairs), 1) < live_ref[0:1]).astype(jnp.float32)
     stick = stick_ref[...].astype(jnp.float32)
     weights = (stiff_ref[...] * live) * (stick + (1.0 - stick) * slip_ref[...])
     low = transform(table_ref, 0, W_LOW, weights[:HALF] - weights[HALF:])
@@ -345,7 +345,7 @@
             jax.ShapeDtypeStruct((ROWS * N_FIRST, LANES), jnp.int32),
             jax.ShapeDtypeStruct((T_ROWS, 2 * LANES), jnp.bfloat16),
         ),
-        in_specs=[pl.BlockSpec(memory_space=pltpu.SMEM)] + [hbm] * 7,
+        in_specs=[vmem] + [hbm] * 7,
         out_specs=(vmem, vmem),
         scratch_shapes=[
             pltpu.VMEM((SAMPLES, pairs), jnp.int32),
@@ -358,7 +358,7 @@
         ],
         compiler_params=params,
     )(
-        live_pairs,
+        jnp.broadcast_to(live_pairs.reshape(1, 1), (8, pairs)),
         in_hbm(stick),
         in_hbm(stiffness.reshape(1, pairs)),
         in_hbm(slip_tangent),

time: 42.9 us -> 42.9 us (level)
  no operation moved by 1% of the time
where the time goes in v11:
time: 42.9 us; the launch traced here: 42.7 us
  blocking collectives  38.4 us (90%)
  Pallas kernels  3.69 us (9%)
  between operations  0.67 us (2%)
    all_to_all x1, blocking collectives, on_device(): lax.all_to_all(slots.reshape(N_FIRST, 1, ROWS * LANES), ('xz', 'c'), 0, 0...  30.2 us
    all_to_all x1, blocking collectives, on_device(): lax.all_to_all(sums.reshape(N_REST * N_HARM, NODE_DEV, LANES), ('c', 'h')...  8.16 us
    pallas_call x1, Pallas kernels, on_device(): pl.pallas_call(send_kernel, out_shape=(jax.ShapeDtypeStruct((ROWS * N_FIR...  1.88 us
    pallas_call x1, Pallas kernels, on_device(): pl.pallas_call(expand_kernel, out_shape=jax.ShapeDtypeStruct((PER, COEFS,...  1.23 us

profile of v11, /device:TPU:1, one launch (start us, length us, event | category | flops | bytes accessed | tf_op | source)
XLA Modules:
  0.0 42.7 jit_solution(17239788675732083438)
XLA Ops:
  0.7 1.9 %shard_map.82 = (s32[320,128]{1,0:T(8,128)S(1)}, bf16[1224,256]{1,0:T(8,128)(2,1)S(1)}) custom-call(s32[8,128]{1,0:T(8,128)S(1)} %broadcast_in_dim.8.live_ref, s32[256,128]{1,0:T(8,128)} %stick_hbm.1, f32[1,128]{1,0:T(1,128)} %bitcast.12, f32[256,128]{1,0:T(8,128)} %slip_hbm.1, f32[256,128]{1,0:T(8,128)} %force_hbm.1, s32[2,128]{1,0:T(2,128)} %owner_hbm.1, ...), custom_call_target="tpu_custom_call" | custom-call | tf_op jit(solution)/shard_map/pallas_call | solution.py:342
  2.6 30.2 %all_to_all.10 = s32[64,1,640]{2,1,0:T(1,128)S(1)} all-to-all(s32[64,1,640]{2,1,0:T(1,128)S(1)} %bitcast.11), channel_id=1, replica_groups={{320,328,336,344,352,360,368,376,256,264,272,280,288,296,304,312,448,45..., dimensions={0} | all-to-all | bytes 327680 | tf_op jit(solution)/shard_map/all_to_all | solution.py:370
  32.8 0.6 %shard_map.83 = s32[256,128]{1,0:T(8,128)S(1)} custom-call(s32[320,128]{1,0:T(8,128)S(1)} %bitcast.8), custom_call_target="tpu_custom_call" | custom-call | tf_op jit(solution)/shard_map/pallas_call | solution.py:378
  33.3 8.2 %all_to_all.11 = s32[8,32,128]{2,1,0:T(8,128)S(1)} all-to-all(s32[8,32,128]{2,1,0:T(8,128)S(1)} %bitcast.9), channel_id=1, replica_groups={{6,7,4,5,2,3,0,1},{14,15,12,13,10,11,8,9},{22,23,20,21,18,19,16,17},{30..., dimensions={0} | all-to-all | bytes 262144 | tf_op jit(solution)/shard_map/all_to_all | solution.py:385
  41.5 1.2 %shard_map.84 = bf16[17,67,128]{2,1,0:T(8,128)(2,1)} custom-call(s32[256,128]{1,0:T(8,128)S(1)} %bitcast.10, bf16[1224,256]{1,0:T(8,128)(2,1)S(1)} %get-tuple-element.8.table_ref), custom_call_target="tpu_custom_call" | custom-call | tf_op jit(solution)/shard_map/pallas_call | solution.py:393
  (1 shorter events, 0.0 us)
